TPU v7x, 128 devices: a whole 4x4x4 slice. The times are simulated.
128 devices in a mesh: dp: 32 (over z, y, core), group: 4 (over x).
Axes of the slice: x: 4, y: 4, z: 4, core: 2. Of those that a mesh axis runs over, the one named last changes fastest.
Arguments:
- tokens: bfloat16 [32768, 1024], P(('dp', 'group')), may hold values from -16 to 16
- cotangent: bfloat16 [32768, 1024], P(('dp', 'group')), may hold values from -6 to 6
- doc_lengths: int32 [32, 4], P('dp'), may hold values from 1 to 896, 1024 in all within a row
- attn_in: float32 [1024, 3072], P(('dp', 'group')), may hold values from -0.1875 to 0.1875
- attn_out: float32 [1024, 1024], P(('dp', 'group')), may hold values from -2 to 2
- ff_in: float32 [1024, 4096], P(('dp', 'group')), may hold values from -0.1875 to 0.1875
- ff_out: float32 [4096, 1024], P(('dp', 'group')), may hold values from -0.09375 to 0.09375
- norm_gains: float32 [1024, 2], P(('dp', 'group')), may hold values from 0.5 to 1.5
- bias_table: float32 [1024, 6], P(('dp', 'group')), may hold values from -3 to 3
- ff_bias: float32 [4096], P(('dp', 'group')), may hold values from -3 to 5
- first_attn_in: float32 [1024, 3072], P(('dp', 'group')), may hold values from -0.0006 to 0.0006
- first_attn_out: float32 [1024, 1024], P(('dp', 'group')), may hold values from -0.0006 to 0.0006
- first_ff_in: float32 [1024, 4096], P(('dp', 'group')), may hold values from -0.0006 to 0.0006
- first_ff_out: float32 [4096, 1024], P(('dp', 'group')), may hold values from -0.0006 to 0.0006
- first_norm_gains: float32 [1024, 2], P(('dp', 'group')), may hold values from -0.0006 to 0.0006
- first_bias_table: float32 [1024, 6], P(('dp', 'group')), may hold values from -0.0006 to 0.0006
- first_ff_bias: float32 [4096], P(('dp', 'group')), may hold values from -0.0006 to 0.0006
- second_attn_in: float32 [1024, 3072], P(('dp', 'group')), may hold values from 1e-10 to 1e-08
- second_attn_out: float32 [1024, 1024], P(('dp', 'group')), may hold values from 1e-10 to 1e-08
- second_ff_in: float32 [1024, 4096], P(('dp', 'group')), may hold values from 1e-10 to 1e-08
- second_ff_out: float32 [4096, 1024], P(('dp', 'group')), may hold values from 1e-10 to 1e-08
- second_norm_gains: float32 [1024, 2], P(('dp', 'group')), may hold values from 1e-10 to 1e-08
- second_bias_table: float32 [1024, 6], P(('dp', 'group')), may hold values from 1e-10 to 1e-08
- second_ff_bias: float32 [4096], P(('dp', 'group')), may hold values from 1e-10 to 1e-08
Outputs:
- block_out: bfloat16 [32768, 1024], P(('dp', 'group'))
- input_grad: float32 [32768, 1024], P(('dp', 'group'))
- grad_attn_in: float32 [1024, 3072], P(('dp', 'group'))
- grad_attn_out: float32 [1024, 1024], P(('dp', 'group'))
- grad_ff_in: float32 [1024, 4096], P(('dp', 'group'))
- grad_ff_out: float32 [4096, 1024], P(('dp', 'group'))
- grad_norm_gains: float32 [1024, 2], P(('dp', 'group'))
- grad_bias_table: float32 [1024, 6], P(('dp', 'group'))
- grad_ff_bias: float32 [4096], P(('dp', 'group'))
- step_attn_in: float32 [1024, 3072], P(('dp', 'group'))
- step_attn_out: float32 [1024, 1024], P(('dp', 'group'))
- step_ff_in: float32 [1024, 4096], P(('dp', 'group'))
- step_ff_out: float32 [4096, 1024], P(('dp', 'group'))
- step_norm_gains: float32 [1024, 2], P(('dp', 'group'))
- step_bias_table: float32 [1024, 6], P(('dp', 'group'))
- step_ff_bias: float32 [4096], P(('dp', 'group'))
Inputs may be any that keep to these rules, and one draw needn't show every extreme that they name: `doc_lengths`: each row lists the lengths of the 4 documents packed in order into one sequence; a row sums to 1024 and its longest document has exactly 896 tokens.
All inputs are finite; a program needn't handle non-finite values.
Results may differ from a plain program's by a relative error of at most 0.015.
The roundings to bfloat16 on the way count: a program that leaves them out, or rounds other values in their place, can miss the bound.
Values may be sent and summed in bfloat16 or wider, within the bound.
No kernel may reach another device: no remote copies, remote signals or barrier semaphores. Data moves between devices by JAX's collectives and lax.ppermute only.
A program may use at most 192 MiB of HBM per device.

v0:
```python
import jax
import jax.numpy as jnp
from jax import lax
from jax.sharding import PartitionSpec as P

HEADS = 16
WINDOW = 1024


NORM_EPS = 1e-06
CLIP_NORM = 1.0
BETA_ONE = 0.9
BETA_TWO = 0.999
STEP_COUNT = 10
ADAM_EPS = 1e-06
WEIGHT_DECAY = 0.01
MASKED_SCORE = -1e30


def shortened(shard):
    return jax.tree.map(lambda a: a.astype(jnp.bfloat16) if a.dtype == jnp.float32 else a, shard)


def layer_norm(values_in, gain_vec, shift_vec):
    center = values_in - jnp.mean(values_in, axis=-1, keepdims=True)
    spread = jnp.mean(center * center, axis=-1, keepdims=True)
    return center * lax.rsqrt(spread + NORM_EPS) * gain_vec + shift_vec


def gelu_tanh(values_in):
    return jax.nn.gelu(values_in, approximate=True)


def doc_ids(lengths, positions):
    doc_ends = jnp.cumsum(lengths)
    return jnp.sum((positions[:, None] >= doc_ends[None, :-1]).astype(jnp.int32), axis=1)


def lamb_step(weight, grad, first_mom, second_mom):
    new_first = BETA_ONE * first_mom + (1.0 - BETA_ONE) * grad
    new_second = BETA_TWO * second_mom + (1.0 - BETA_TWO) * grad * grad
    direction = (
        new_first
        / (1.0 - BETA_ONE**STEP_COUNT)
        / (jnp.sqrt(new_second / (1.0 - BETA_TWO**STEP_COUNT)) + ADAM_EPS)
        + WEIGHT_DECAY * weight
    )
    weight_norm = jnp.sqrt(jnp.sum(weight * weight))
    dir_norm = jnp.sqrt(jnp.sum(direction * direction))
    return direction * (weight_norm / jnp.maximum(dir_norm, 1.0))


def body(
    tokens,
    cotangent,
    doc_lengths,
    attn_in,
    attn_out,
    ff_in,
    ff_out,
    norm_gains,
    bias_table,
    ff_bias,
    first_attn_in,
    first_attn_out,
    first_ff_in,
    first_ff_out,
    first_norm_gains,
    first_bias_table,
    first_ff_bias,
    second_attn_in,
    second_attn_out,
    second_ff_in,
    second_ff_out,
    second_norm_gains,
    second_bias_table,
    second_ff_bias,
):
    shards = (attn_in, attn_out, ff_in, ff_out, norm_gains, bias_table, ff_bias)
    firsts = (
        first_attn_in,
        first_attn_out,
        first_ff_in,
        first_ff_out,
        first_norm_gains,
        first_bias_table,
        first_ff_bias,
    )
    seconds = (
        second_attn_in,
        second_attn_out,
        second_ff_in,
        second_ff_out,
        second_norm_gains,
        second_bias_table,
        second_ff_bias,
    )
    lowered = tuple((weight.astype(jnp.bfloat16) for weight in shards))
    group_size = lax.axis_size("group")
    gathered = jax.tree.map(
        lambda part, own: part.astype(own.dtype),
        lax.all_gather(shortened(lowered), ("dp", "group"), axis=0, tiled=True),
        lowered,
    )
    w_in, w_out, w_up, w_down, gain_low, bias_low, ffb_low = gathered
    gain_f = gain_low.astype(jnp.float32)
    bias_f = bias_low.astype(jnp.float32)
    ffb_f = ffb_low.astype(jnp.float32)
    tok_rows, model_width = tokens.shape
    seq_len = tok_rows * group_size
    head_count = HEADS
    head_size = model_width // head_count
    score_scale = head_size ** (-0.5)
    first_row = lax.axis_index("group") * tok_rows
    own_pos = first_row + jnp.arange(tok_rows, dtype=jnp.int32)
    all_pos = jnp.arange(seq_len, dtype=jnp.int32)
    lengths = doc_lengths[0]
    own_ids = doc_ids(lengths, own_pos)
    all_ids = doc_ids(lengths, all_pos)
    visible = (own_ids[:, None] == all_ids[None, :]) & (
        jnp.abs(own_pos[:, None] - all_pos[None, :]) < WINDOW // 2
    )
    zero_col = jnp.zeros((model_width,), jnp.float32)
    in_bias = jnp.concatenate([bias_f[:, 0], zero_col, bias_f[:, 1]])
    qkv = (jnp.dot(tokens, w_in, preferred_element_type=jnp.float32) + in_bias).astype(jnp.bfloat16)
    query = qkv[:, :model_width]
    key_own = qkv[:, model_width : 2 * model_width]
    value_own = qkv[:, 2 * model_width :]
    key_all, value_all = (
        lax.all_gather(key_own, "group", axis=0, tiled=True),
        lax.all_gather(value_own, "group", axis=0, tiled=True),
    )
    query_heads = query.reshape(tok_rows, head_count, head_size)
    key_heads = key_all.reshape(seq_len, head_count, head_size)
    value_heads = value_all.reshape(seq_len, head_count, head_size)

    def masked_scores():
        raw_scores = (
            jnp.einsum("thd,shd->hts", query_heads, key_heads, preferred_element_type=jnp.float32)
            * score_scale
        )
        return jnp.where(visible[None], raw_scores, MASKED_SCORE)

    scores = masked_scores()
    row_top = jnp.max(scores, axis=-1, keepdims=True)
    row_total = jnp.log(jnp.sum(jnp.exp(scores - row_top), axis=-1, keepdims=True)) + row_top
    probs_low = jnp.exp(scores - row_total).astype(jnp.bfloat16)
    context = (
        jnp.einsum("hts,shd->thd", probs_low, value_heads, preferred_element_type=jnp.float32)
        .reshape(tok_rows, model_width)
        .astype(jnp.bfloat16)
    )
    attended = jnp.dot(context, w_out, preferred_element_type=jnp.float32) + bias_f[:, 2]
    first, norm_one_pull = jax.vjp(
        layer_norm, tokens.astype(jnp.float32) + attended, gain_f[:, 0], bias_f[:, 3]
    )
    first_low = first.astype(jnp.bfloat16)
    hidden = jnp.dot(first_low, w_up, preferred_element_type=jnp.float32) + ffb_f
    active, gelu_pull = jax.vjp(gelu_tanh, hidden)
    active_low = active.astype(jnp.bfloat16)
    branch = jnp.dot(active_low, w_down, preferred_element_type=jnp.float32) + bias_f[:, 4]
    output, norm_two_pull = jax.vjp(layer_norm, first + branch, gain_f[:, 1], bias_f[:, 5])
    block_out = output.astype(jnp.bfloat16)
    d_two, d_gain_two, d_shift_two = norm_two_pull(cotangent.astype(jnp.float32))
    d_branch = d_two.astype(jnp.bfloat16)
    grad_down = jnp.einsum("tf,td->fd", active_low, d_branch, preferred_element_type=jnp.float32)
    d_active = jnp.einsum("td,fd->tf", d_branch, w_down, preferred_element_type=jnp.float32)
    (d_hidden,) = gelu_pull(d_active)
    d_hidden_low = d_hidden.astype(jnp.bfloat16)
    grad_up = jnp.einsum("td,tf->df", first_low, d_hidden_low, preferred_element_type=jnp.float32)
    d_first = d_two + jnp.einsum(
        "tf,df->td", d_hidden_low, w_up, preferred_element_type=jnp.float32
    )
    d_one, d_gain_one, d_shift_one = norm_one_pull(d_first)
    d_attended = d_one.astype(jnp.bfloat16)
    grad_out = jnp.einsum("td,te->de", context, d_attended, preferred_element_type=jnp.float32)
    d_context = jnp.einsum(
        "te,de->td", d_attended, w_out, preferred_element_type=jnp.float32
    ).astype(jnp.bfloat16)
    d_context_heads = d_context.reshape(tok_rows, head_count, head_size)
    attn_probs = jnp.exp(masked_scores() - row_total)
    d_probs = jnp.einsum(
        "thd,shd->hts", d_context_heads, value_heads, preferred_element_type=jnp.float32
    )
    row_delta = jnp.sum(attn_probs * d_probs, axis=-1, keepdims=True)
    d_scores = (attn_probs * (d_probs - row_delta)).astype(jnp.bfloat16)
    d_query = (
        (
            jnp.einsum("hts,shd->thd", d_scores, key_heads, preferred_element_type=jnp.float32)
            * score_scale
        )
        .reshape(tok_rows, model_width)
        .astype(jnp.bfloat16)
    )
    d_key_all = (
        jnp.einsum("hts,thd->shd", d_scores, query_heads, preferred_element_type=jnp.float32)
        * score_scale
    ).reshape(seq_len, model_width)
    d_value_all = jnp.einsum(
        "hts,thd->shd",
        attn_probs.astype(jnp.bfloat16),
        d_context_heads,
        preferred_element_type=jnp.float32,
    ).reshape(seq_len, model_width)
    d_key, d_value = (
        lax.psum_scatter(
            d_key_all.astype(jnp.bfloat16), "group", scatter_dimension=0, tiled=True
        ).astype(jnp.float32),
        lax.psum_scatter(
            d_value_all.astype(jnp.bfloat16), "group", scatter_dimension=0, tiled=True
        ).astype(jnp.float32),
    )
    d_key_low = d_key.astype(jnp.bfloat16)
    d_value_low = d_value.astype(jnp.bfloat16)
    d_qkv = jnp.concatenate([d_query, d_key_low, d_value_low], axis=1)
    grad_in = jnp.einsum("td,te->de", tokens, d_qkv, preferred_element_type=jnp.float32)
    input_grad = d_one + jnp.einsum("te,de->td", d_qkv, w_in, preferred_element_type=jnp.float32)
    grad_gains = jnp.stack([d_gain_one, d_gain_two], axis=1)
    grad_biases = jnp.stack(
        [
            jnp.sum(d_query.astype(jnp.float32), axis=0),
            jnp.sum(d_value_low.astype(jnp.float32), axis=0),
            jnp.sum(d_attended.astype(jnp.float32), axis=0),
            d_shift_one,
            jnp.sum(d_branch.astype(jnp.float32), axis=0),
            d_shift_two,
        ],
        axis=1,
    )
    grad_ffb = jnp.sum(d_hidden_low.astype(jnp.float32), axis=0)
    partial_grads = (grad_in, grad_out, grad_up, grad_down, grad_gains, grad_biases, grad_ffb)
    grads = (
        lax.psum_scatter(partial_grads[0], ("dp", "group"), scatter_dimension=0, tiled=True),
        lax.psum_scatter(partial_grads[1], ("dp", "group"), scatter_dimension=0, tiled=True),
        lax.psum_scatter(partial_grads[2], ("dp", "group"), scatter_dimension=0, tiled=True),
        lax.psum_scatter(partial_grads[3], ("dp", "group"), scatter_dimension=0, tiled=True),
        lax.psum_scatter(partial_grads[4], ("dp", "group"), scatter_dimension=0, tiled=True),
        lax.psum_scatter(partial_grads[5], ("dp", "group"), scatter_dimension=0, tiled=True),
        lax.psum_scatter(partial_grads[6], ("dp", "group"), scatter_dimension=0, tiled=True),
    )
    local_squares = sum((jnp.sum(grad * grad) for grad in grads))
    all_squares = lax.psum(local_squares, ("dp", "group"))
    factor = CLIP_NORM / jnp.maximum(jnp.sqrt(all_squares), CLIP_NORM)
    steps = tuple(
        (
            lamb_step(weight, grad * factor, first_mom, second_mom)
            for weight, grad, first_mom, second_mom in zip(shards, grads, firsts, seconds)
        )
    )
    return (
        block_out,
        input_grad,
        grads[0],
        grads[1],
        grads[2],
        grads[3],
        grads[4],
        grads[5],
        grads[6],
        steps[0],
        steps[1],
        steps[2],
        steps[3],
        steps[4],
        steps[5],
        steps[6],
    )


def solution(mesh):
    return jax.shard_map(
        body,
        mesh=mesh,
        in_specs=(
            P(("dp", "group"), None),
            P(("dp", "group"), None),
            P("dp", None),
            P(("dp", "group"), None),
            P(("dp", "group"), None),
            P(("dp", "group"), None),
            P(("dp", "group"), None),
            P(("dp", "group"), None),
            P(("dp", "group"), None),
            P(("dp", "group")),
            P(("dp", "group"), None),
            P(("dp", "group"), None),
            P(("dp", "group"), None),
            P(("dp", "group"), None),
            P(("dp", "group"), None),
            P(("dp", "group"), None),
            P(("dp", "group")),
            P(("dp", "group"), None),
            P(("dp", "group"), None),
            P(("dp", "group"), None),
            P(("dp", "group"), None),
            P(("dp", "group"), None),
            P(("dp", "group"), None),
            P(("dp", "group")),
        ),
        out_specs=(
            P(("dp", "group"), None),
            P(("dp", "group"), None),
            P(("dp", "group"), None),
            P(("dp", "group"), None),
            P(("dp", "group"), None),
            P(("dp", "group"), None),
            P(("dp", "group"), None),
            P(("dp", "group"), None),
            P(("dp", "group")),
            P(("dp", "group"), None),
            P(("dp", "group"), None),
            P(("dp", "group"), None),
            P(("dp", "group"), None),
            P(("dp", "group"), None),
            P(("dp", "group"), None),
            P(("dp", "group")),
        ),
        check_vma=False,
    )
```

profile of v0, /device:TPU:34, one launch (start us, length us, event | category | flops | bytes accessed | tf_op | source)
XLA Modules:
  0.0 2764.9 jit_solution(3562080587917823915)
XLA Ops:
  7.2 2.3 multiply_reduce_fusion.13
  9.6 1.4 multiply_reduce_fusion.18
  11.0 60.7 %all_gather.28 = bf16[1024,6]{1,0:T(8,128)(2,1)S(1)} all-gather(bf16[8,6]{1,0:T(8,128)(2,1)S(1)} %get-tuple-element.156), channel_id=1, replica_groups=mesh['dp'=32,'group'=4] {'dp','group'}, dimensions={0}, use_global_device_ids=true | all-gather | bytes 12384 | tf_op jit(solution)/shard_map/all_gather | solution.py:102
  71.7 1.6 slice_reduce_fusion
  73.4 6.2 all-gather.8.cloned.1.call-done
  79.6 4.6 fusion.9
  84.3 1.1 fusion.75
  85.5 0.7 all-gather.10.cloned.1.call-update
  86.2 1.2 multiply_reduce_fusion.15
  87.5 1.3 multiply_reduce_fusion.9
  88.9 1.2 multiply_reduce_fusion.7
  91.0 64.8 %all-reduce = bf16[4096]{0:T(1024)(128)(2,1)S(1)} all-reduce(bf16[4096]{0:T(1024)(128)(2,1)S(1)} %dynamic-update-slice), channel_id=1, replica_groups=mesh['dp'=32,'group'=4] {'dp','group'}, use_global_device_ids=true, to_apply=%add | all-reduce | flops 4096 | bytes 16384
  157.1 44.8 %all-gather = bf16[128,8,2]{1,2,0:T(2,128)(2,1)S(1)} all-gather(bf16[1,8,2]{1,2,0:T(2,128)(2,1)S(1)} %get-tuple-element.158), channel_id=1, replica_groups=mesh['dp'=32,'group'=4] {'dp','group'}, dimensions={0}, use_global_device_ids=true | all-gather | bytes 4128 | tf_op jit(solution)/shard_map/all_gather | solution.py:102
  203.2 3.0 copy.144
  206.3 4.0 copy.142
  210.3 3.0 fusion
  213.3 4.4 exponential_reduce_fusion
  217.7 1.9 copy-done
  219.6 5.7 convolution_convert_fusion.1
  225.3 2.7 fusion.77
  229.4 58.4 %all-gather.16.cloned.1.call-done = bf16[1024,4096]{1,0:T(8,128)(2,1)} async-done(((bf16[8,4096]{1,0:T(8,128)(2,1)}), bf16[1024,4096]{1,0:T(8,128)(2,1)}) %all-gather.16.cloned.1.call-update) | async-done | bytes 8388624 | tf_op jit(solution)/shard_map/all_gather | solution.py:102
  287.8 7.8 convolution_add_fusion
  295.6 63.5 %all-gather.18.cloned.1.call-done = bf16[4096,1024]{1,0:T(8,128)(2,1)} async-done(((bf16[32,1024]{1,0:T(8,128)(2,1)}), bf16[4096,1024]{1,0:T(8,128)(2,1)}) %all-gather.18.cloned.1.call-update) | async-done | bytes 8388624 | tf_op jit(solution)/shard_map/all_gather | solution.py:102
  359.1 7.6 fusion.78
  366.9 1.0 fusion.16
  368.0 1.3 fusion.74
  369.2 0.8 convert_reduce_fusion.2
  370.0 5.7 convert_reduce_fusion
  375.8 3.5 multiply_reduce_fusion.2
  379.7 0.9 copy-done.6
  380.6 0.8 convert_reduce_fusion.3
  381.4 0.8 copy-done.14
  382.2 1.5 convolution_convert_fusion.2
  383.7 2.0 copy.147
  385.8 11.3 convolution_convert_fusion
  397.1 13.8 multiply_reduce_fusion
  410.9 12.4 multiply_convert_fusion
  423.4 3.5 multiply_convert_fusion.1
  427.3 3.9 fusion.79
  431.3 6.9 convert_reduce_fusion.5
  438.1 19.1 reduce-scatter.11.cloned.1.call-done
  457.2 7.9 convolution_bitcast_fusion
  465.1 12.6 copy.155
  478.0 1.3 copy-done.17
  479.3 8.2 fusion.63
  487.6 1.0 copy-done.13
  488.6 10.7 fusion.66
  505.6 66.0 %all-reduce.4 = (f32[1024,2]{0,1:T(2,128)S(1)}, f32[1024,6]{0,1:T(8,128)S(1)}, f32[4096]{0:T(1024)S(1)}) all-reduce(f32[1024,2]{0,1:T(2,128)S(1)} %pad_maximum_fusion.4, f32[1024,6]{0,1:T(8,128)S(1)} %stack.39, f32[4096]{0:T(1024)S(1)} %copy-done.39), channel_id=8, replica_groups=mesh['dp'=32,'group'=4] {'dp','group'}, use_global_device_ids=true, to_apply=%region_22.23.clone | all-reduce | flops 12288 | bytes 98304
  573.7 5.7 convolution_add_fusion.3
  579.4 444.2 %reduce-scatter.15.cloned.1.call-done = f32[8,1024]{1,0:T(8,128)} async-done(((f32[1024,1024]{1,0:T(8,128)}), f32[8,1024]{1,0:T(8,128)}) %reduce-scatter.15.cloned.1.call-update) | async-done | bytes 32784 | tf_op jit(solution)/shard_map/reduce_scatter | solution.py:234
  1023.6 1.4 multiply_reduce_fusion.16
  1025.0 301.4 %reduce-scatter.21.cloned.1.call-done = f32[8,3072]{1,0:T(8,128)} async-done(((f32[1024,3072]{1,0:T(8,128)}), f32[8,3072]{1,0:T(8,128)}) %reduce-scatter.21.cloned.1.call-update) | async-done | bytes 98320
  1326.4 1.4 copy.156
  1327.8 1.0 multiply_reduce_fusion.1
  1330.1 591.4 %reduce-scatter.17.cloned.1.call-done = f32[8,4096]{1,0:T(8,128)} async-done(((f32[1024,4096]{1,0:T(8,128)}), f32[8,4096]{1,0:T(8,128)}) %reduce-scatter.17.cloned.1.call-update) | async-done | bytes 131088 | tf_op jit(solution)/shard_map/reduce_scatter | solution.py:235
  1921.5 1.5 multiply_reduce_fusion.11
  1923.7 669.1 %reduce-scatter.19.cloned.1.call-done = f32[32,1024]{1,0:T(8,128)} async-done(((f32[4096,1024]{1,0:T(8,128)}), f32[32,1024]{1,0:T(8,128)}) %reduce-scatter.19.cloned.1.call-update) | async-done | bytes 131088 | tf_op jit(solution)/shard_map/reduce_scatter | solution.py:236
  2592.8 1.5 multiply_reduce_fusion.10
  2597.7 141.5 %psum.7 = f32[]{:T(128)} all-reduce(f32[]{:T(128)S(6)} %add.285), channel_id=1, replica_groups=mesh['dp'=32,'group'=4] {'dp','group'}, use_global_device_ids=true, to_apply=%region_39.40 | all-reduce | flops 1 | bytes 8 | tf_op jit(solution)/shard_map/psum | solution.py:242
  2741.3 0.7 copy.154
  2744.7 1.4 multiply_reduce_fusion.14
  2746.8 1.7 multiply_reduce_fusion.12
  2749.2 1.6 multiply_reduce_fusion.6
  2751.5 1.6 multiply_reduce_fusion.8
  (204 shorter events, 16.5 us)
Async XLA Ops:
  7.2 72.4 %copy-start.8 = (bf16[256,1024]{1,0:T(8,128)(2,1)S(1)}, bf16[256,1024]{1,0:T(8,128)(2,1)}, u32[]{:S(2)}) copy-start(bf16[256,1024]{1,0:T(8,128)(2,1)} %param.24) | copy-start | bytes 1572868
  7.2 72.4 %all-gather.8.cloned.1.call-start = ((), (), s32[]{:S(2)}) async-start(), calls=%async_computation.6 | async-start | bytes 6340608 | tf_op jit(solution)/shard_map/all_gather | solution.py:102
  9.5 193.7 %all-gather.12.cloned.1.call-start = ((), (), s32[]{:S(2)}) async-start(), calls=%async_computation.8 | async-start | bytes 2621440 | tf_op jit(solution)/shard_map/all_gather | solution.py:130
  84.2 4.6 copy-start.19
  84.2 5.9 copy-start.55
  84.2 72.2 %copy-start.47 = (f32[8,2]{0,1:T(2,128)S(1)}, f32[8,2]{0,1:T(2,128)}, u32[]{:S(2)}) copy-start(f32[8,2]{0,1:T(2,128)} %param.31) | copy-start | bytes 196
  84.3 117.9 %copy-start.59 = (s32[1,4]{1,0:T(1,128)S(1)}, s32[1,4]{1,0:T(1,128)}, u32[]{:S(2)}) copy-start(s32[1,4]{1,0:T(1,128)} %param.26) | copy-start | bytes 52
  85.4 120.9 %all-gather.10.cloned.1.call-start = ((), (), s32[]{:S(2)}) async-start(), calls=%async_computation.7 | async-start | bytes 2621440 | tf_op jit(solution)/shard_map/all_gather | solution.py:131
  86.2 139.2 %all-gather.14.cloned.1.call-start = ((), (), s32[]{:S(2)}) async-start(), calls=%async_computation.9 | async-start | bytes 2113536 | tf_op jit(solution)/shard_map/all_gather | solution.py:102
  87.5 200.4 %all-gather.16.cloned.1.call-start = ((), (), s32[]{:S(2)}) async-start(), calls=%async_computation.10 | async-start | bytes 8454144 | tf_op jit(solution)/shard_map/all_gather | solution.py:102
  88.8 270.3 %all-gather.18.cloned.1.call-start = ((), (), s32[]{:S(2)}) async-start(), calls=%async_computation.11 | async-start | bytes 8454144 | tf_op jit(solution)/shard_map/all_gather | solution.py:102
  90.1 348.0 %reduce-scatter.13.cloned.1.call-start = ((), (), s32[]{:S(2)}) async-start(), calls=%async_computation.13 | async-start | bytes 2621440 | tf_op jit(solution)/shard_map/reduce_scatter | solution.py:209
  203.2 7.1 copy-start.3
  213.3 6.3 copy-start
  213.3 6.3 copy-start.2
  217.7 7.6 copy-start.23
  359.1 10.9 slice-start.2
  359.1 7.9 copy-start.15
  359.1 8.9 copy-start.34
  359.1 10.9 slice-start.3
  366.7 3.4 copy-start.5
  369.2 6.5 slice-start
  370.0 5.7 copy-start.12
  370.0 5.7 copy-start.33
  370.0 5.7 slice-start.1
  375.7 3.5 copy-start.16
  375.7 3.5 copy-start.42
  397.1 60.2 %reduce-scatter.11.cloned.1.call-start = ((), (), s32[]{:S(2)}) async-start(), calls=%async_computation.12 | async-start | bytes 2621440 | tf_op jit(solution)/shard_map/reduce_scatter | solution.py:206
  397.1 13.8 copy-start.24
  410.9 12.4 copy-start.4
  423.3 3.9 copy-start.1
  427.2 596.4 %reduce-scatter.15.cloned.1.call-start = ((), (), s32[]{:S(2)}) async-start(), calls=%async_computation.14 | async-start | bytes 4227072 | tf_op jit(solution)/shard_map/reduce_scatter | solution.py:234
  431.2 895.2 %reduce-scatter.21.cloned.1.call-start = ((), (), s32[]{:S(2)}) async-start(), calls=%async_computation.17 | async-start | bytes 12681216
  477.7 1443.8 %reduce-scatter.17.cloned.1.call-start = ((), (), s32[]{:S(2)}) async-start(), calls=%async_computation.15 | async-start | bytes 16908288 | tf_op jit(solution)/shard_map/reduce_scatter | solution.py:235
  487.5 2105.3 %reduce-scatter.19.cloned.1.call-start = ((), (), s32[]{:S(2)}) async-start(), calls=%async_computation.16 | async-start | bytes 16908288 | tf_op jit(solution)/shard_map/reduce_scatter | solution.py:236
  499.3 5.9 copy-start.38
  499.3 5.9 copy-start.49
  499.3 5.9 copy-start.11
  499.3 6.1 copy-start.35
  499.3 6.1 copy-start.36
  499.3 6.1 copy-start.37
  499.3 6.1 copy-start.43
  499.4 6.2 copy-start.39
  499.4 74.2 %copy-start.7 = (f32[256,1024]{1,0:T(8,128)S(1)}, f32[256,1024]{1,0:T(8,128)}, u32[]{:S(2)}) copy-start(f32[256,1024]{1,0:T(8,128)} %copy-done.6) | copy-start | bytes 3145732
  499.4 74.2 %copy-start.9 = (bf16[16,64,256]{2,1,0:T(8,128)(2,1)S(1)}, bf16[16,64,256]{2,1,0:T(8,128)(2,1)}, u32[]{:S(2)}) copy-start(bf16[16,64,256]{2,1,0:T(8,128)(2,1)} %get-tuple-element.171) | copy-start | bytes 1572868
  499.4 74.1 %copy-start.18 = (bf16[256,1024]{0,1:T(8,128)(2,1)S(1)}, bf16[256,1024]{0,1:T(8,128)(2,1)}, u32[]{:S(2)}) copy-start(bf16[256,1024]{0,1:T(8,128)(2,1)} %reduce-scatter.11.cloned.1.call-done) | copy-start | bytes 1572868
  499.4 74.1 %copy-start.51 = (f32[256]{0:T(256)S(1)}, f32[256]{0:T(256)}, u32[]{:S(2)}) copy-start(f32[256]{0:T(256)} %copy-done.50) | copy-start | bytes 3076
  572.2 2169.8 %copy-start.52 = (f32[32]{0:T(128)}, f32[32]{0:T(128)S(1)}, u32[]{:S(2)}) copy-start(f32[32]{0:T(128)S(1)} %get-tuple-element.126) | copy-start | bytes 388
  572.9 2170.4 %copy-start.46 = (f32[8,2]{0,1:T(2,128)}, f32[8,2]{0,1:T(2,128)S(1)}, u32[]{:S(2)}) copy-start(f32[8,2]{0,1:T(2,128)S(1)} %get-tuple-element.130) | copy-start | bytes 196
  573.5 2168.4 %copy-start.56 = (f32[32]{0:T(128)S(1)}, f32[32]{0:T(128)}, u32[]{:S(2)}) copy-start(f32[32]{0:T(128)} %param.33) | copy-start | bytes 388
  573.6 2168.4 %copy-start.57 = (f32[32]{0:T(128)S(1)}, f32[32]{0:T(128)}, u32[]{:S(2)}) copy-start(f32[32]{0:T(128)} %param.47) | copy-start | bytes 388
  573.6 2168.4 %copy-start.58 = (f32[32]{0:T(128)S(1)}, f32[32]{0:T(128)}, u32[]{:S(2)}) copy-start(f32[32]{0:T(128)} %param.40) | copy-start | bytes 388
  573.6 2169.7 %copy-start.48 = (f32[8,2]{0,1:T(2,128)S(1)}, f32[8,2]{0,1:T(2,128)}, u32[]{:S(2)}) copy-start(f32[8,2]{0,1:T(2,128)} %param.31) | copy-start | bytes 196
  573.6 2169.7 %copy-start.53 = (f32[8,2]{0,1:T(2,128)S(1)}, f32[8,2]{0,1:T(2,128)}, u32[]{:S(2)}) copy-start(f32[8,2]{0,1:T(2,128)} %param.45) | copy-start | bytes 196
  573.6 2169.7 %copy-start.54 = (f32[8,2]{0,1:T(2,128)S(1)}, f32[8,2]{0,1:T(2,128)}, u32[]{:S(2)}) copy-start(f32[8,2]{0,1:T(2,128)} %param.38) | copy-start | bytes 196
  573.6 2171.0 %copy-start.30 = (f32[8,1024]{1,0:T(8,128)S(1)}, f32[8,1024]{1,0:T(8,128)}, u32[]{:S(2)}) copy-start(f32[8,1024]{1,0:T(8,128)} %param.28) | copy-start | bytes 98308
  573.6 2171.0 %copy-start.31 = (f32[8,1024]{1,0:T(8,128)S(1)}, f32[8,1024]{1,0:T(8,128)}, u32[]{:S(2)}) copy-start(f32[8,1024]{1,0:T(8,128)} %param.42) | copy-start | bytes 98308
  573.6 2171.0 %copy-start.32 = (f32[8,1024]{1,0:T(8,128)S(1)}, f32[8,1024]{1,0:T(8,128)}, u32[]{:S(2)}) copy-start(f32[8,1024]{1,0:T(8,128)} %param.35) | copy-start | bytes 98308
  573.7 2173.1 %copy-start.22 = (f32[8,3072]{1,0:T(8,128)S(1)}, f32[8,3072]{1,0:T(8,128)}, u32[]{:S(2)}) copy-start(f32[8,3072]{1,0:T(8,128)} %param.27) | copy-start | bytes 294916
  579.3 2169.8 %copy-start.25 = (f32[32,1024]{1,0:T(8,128)S(1)}, f32[32,1024]{1,0:T(8,128)}, u32[]{:S(2)}) copy-start(f32[32,1024]{1,0:T(8,128)} %param.44) | copy-start | bytes 393220
  579.3 2169.8 %copy-start.26 = (f32[32,1024]{1,0:T(8,128)S(1)}, f32[32,1024]{1,0:T(8,128)}, u32[]{:S(2)}) copy-start(f32[32,1024]{1,0:T(8,128)} %param.37) | copy-start | bytes 393220
  579.3 2172.1 %copy-start.21 = (f32[8,4096]{1,0:T(8,128)S(1)}, f32[8,4096]{1,0:T(8,128)}, u32[]{:S(2)}) copy-start(f32[8,4096]{1,0:T(8,128)} %param.29) | copy-start | bytes 393220
  579.3 2172.1 %copy-start.27 = (f32[8,4096]{1,0:T(8,128)S(1)}, f32[8,4096]{1,0:T(8,128)}, u32[]{:S(2)}) copy-start(f32[8,4096]{1,0:T(8,128)} %param.43) | copy-start | bytes 393220
  579.4 2172.1 %copy-start.28 = (f32[8,4096]{1,0:T(8,128)S(1)}, f32[8,4096]{1,0:T(8,128)}, u32[]{:S(2)}) copy-start(f32[8,4096]{1,0:T(8,128)} %param.36) | copy-start | bytes 393220
  (12 other events, 21.6 us)
Sparse Core Ops, SparseCore 0:
  11.6 67.9 all-gather.7
  85.5 30.2 all-gather.11
  118.1 30.8 all-gather.9
  152.4 64.0 all-gather.13
  220.1 67.6 all-gather.15
  291.4 67.6 all-gather.17
  397.2 28.0 reduce-scatter.12
  427.8 29.3 reduce-scatter.10
  460.2 563.3 reduce-scatter.14
  1029.8 296.5 reduce-scatter.20
  1329.5 591.9 reduce-scatter.16
  1924.5 668.3 reduce-scatter.18
where the time goes:
time: 2770 us; the launch traced here: 2760 us
  waiting for transfers between devices  2150 us (78%)
  blocking collectives  378 us (14%)
  matrix products  114 us (4%)
  other arithmetic  51.7 us (2%)
  local copies, waits for them, and re-layouts  35.8 us (1%)
  between operations  30.7 us (1%)
    reduce_scatter x1, waiting for transfers between devices, body(): lax.psum_scatter(partial_grads[3], ('dp', 'group'), scatter_dimension=0,...  669 us
    reduce_scatter x1, waiting for transfers between devices, body(): lax.psum_scatter(partial_grads[2], ('dp', 'group'), scatter_dimension=0,...  591 us
    reduce_scatter x1, waiting for transfers between devices, body(): lax.psum_scatter(partial_grads[1], ('dp', 'group'), scatter_dimension=0,...  444 us
    unnamed x13, waiting for transfers between devices  302 us
    psum x1, blocking collectives, body(): all_squares = lax.psum(local_squares, ('dp', 'group'))  141 us
    unnamed x2, blocking collectives  131 us
    all_gather x4, waiting for transfers between devices, body(): lax.all_gather(shortened(lowered), ('dp', 'group'), axis=0, tiled=True)  128 us
    all_gather x2, blocking collectives, body(): lax.all_gather(shortened(lowered), ('dp', 'group'), axis=0, tiled=True)  106 us
  transfers between devices with their start and end apart: 12, of which 8 were waited for; matrix products, arithmetic and copies ran while one was open for 5% of the time, Pallas kernels for 0%

commit v1 on v0

v1 whole, which is shorter than its diff:
```python
import jax
import jax.numpy as jnp
from jax import lax
from jax.experimental import pallas as pl
from jax.experimental.pallas import tpu as pltpu
from jax.sharding import PartitionSpec as P

HEADS = 16
WINDOW = 1024
AXES = ("dp", "group")
RADIX = {"z": 4, "y": 4, "core": 2, "x": 4}

NORM_EPS = 1e-06
CLIP_NORM = 1.0
BETA_ONE = 0.9
BETA_TWO = 0.999
STEP_COUNT = 10
ADAM_EPS = 1e-06
WEIGHT_DECAY = 0.01
MASKED_SCORE = -1e30
F32 = jnp.float32
BF16 = jnp.bfloat16


def pair_list(axis, shift):
    out = []
    for flat in range(128):
        at = {"z": flat // 32, "y": flat // 8 % 4, "core": flat // 4 % 2, "x": flat % 4}
        at[axis] = (at[axis] + shift) % RADIX[axis]
        out.append((flat, ((at["z"] * 4 + at["y"]) * 2 + at["core"]) * 4 + at["x"]))
    return out


def push(value, axis, shift):
    return lax.ppermute(value, AXES, pair_list(axis, shift))


def pick(value, index, dim):
    return lax.dynamic_index_in_dim(value, index, dim, keepdims=False)


def rolled(parts, me, dim):
    joined = jnp.concatenate(parts + parts[:3], axis=dim)
    width = parts[0].shape[dim]
    return lax.dynamic_slice_in_dim(joined, (4 - me) % 4 * width, 4 * width, dim)


def gather_small(value, axis, me, dim):
    value = jnp.expand_dims(value, dim)
    return rolled([value] + [push(value, axis, -j) for j in (1, 2, 3)], me, dim)


def gather_last(value, axis, me, core, buffer, dim, half):
    def put(buf, piece, place, start=0):
        other = push(piece, "core", 1)
        for data, side in ((piece, core), (other, 1 - core)):
            data = jnp.expand_dims(jnp.expand_dims(data, 1), dim if dim != 1 else 1)
            at = [0] * 6
            at[2] = side
            at[dim] = place
            at[half] = start
            buf = lax.dynamic_update_slice(buf, data, tuple(at))
        return buf

    near_up = push(value, axis, -1)
    near_down = push(value, axis, 1)
    buffer = put(buffer, value, me)
    cut = value.shape[0] // 2
    far_one = push(near_up[:cut], axis, -1)
    far_two = push(near_down[cut:], axis, 1)
    buffer = put(buffer, near_up, (me + 1) % 4)
    buffer = put(buffer, near_down, (me + 3) % 4)
    buffer = put(buffer, far_one, (me + 2) % 4)
    return put(buffer, far_two, (me + 2) % 4, cut)


def core_sum(partial, core):
    other = push(pick(partial, 1 - core, 2), "core", 1)
    return (pick(partial, core, 2).astype(F32) + other.astype(F32)).astype(BF16)


def scatter_direct(value, axis, me, dim, dtype):
    total = pick(value, me, dim).astype(F32)
    for k in (1, 3, 2):
        total = total + push(pick(value, (me + k) % 4, dim), axis, k).astype(F32)
    return total.astype(dtype)


def scatter_two(value, axis, me, dim, dtype):
    far = pick(value, (me + 2) % 4, dim)
    cut = far.shape[0] // 2
    from_down = push(far[:cut], axis, 1)
    from_up = push(far[cut:], axis, -1)
    up = pick(value, (me + 1) % 4, dim)
    down = pick(value, (me + 3) % 4, dim)
    up = jnp.concatenate([(up[:cut].astype(F32) + from_down.astype(F32)).astype(BF16), up[cut:]], axis=0)
    down = jnp.concatenate([down[:cut], (down[cut:].astype(F32) + from_up.astype(F32)).astype(BF16)], axis=0)
    got_one = push(up, axis, 1)
    got_two = push(down, axis, -1)
    return (pick(value, me, dim).astype(F32) + got_one.astype(F32) + got_two.astype(F32)).astype(dtype)


def sum_all(value, axes):
    for axis in axes:
        total = value
        for k in range(1, RADIX[axis]):
            total = total + push(value, axis, k)
        value = total
    return value


def scores_of(query, key, code_col, code_row):
    raw = lax.dot_general(query, key, (((1,), (1,)), ((), ())), preferred_element_type=F32)
    return jnp.where(jnp.abs(code_col - code_row) < WINDOW // 2, raw, MASKED_SCORE)


def attend_kernel(q_ref, k_ref, v_ref, col_ref, row_ref, out_ref, lse_ref):
    code_row = row_ref[...]
    for head in range(2):
        lanes = slice(head * 64, head * 64 + 64)
        key = k_ref[:, lanes]
        value = v_ref[:, lanes]
        for block in range(4):
            rows = slice(block * 256, block * 256 + 256)
            query = q_ref[rows, lanes] * BF16(0.125)
            scores = scores_of(query, key, col_ref[rows, :], code_row)
            top = jnp.max(scores, axis=1, keepdims=True)
            raised = jnp.exp(scores - top)
            total = jnp.sum(raised, axis=1, keepdims=True)
            probs = (raised * (1.0 / total)).astype(BF16)
            out_ref[rows, lanes] = jnp.dot(probs, value, preferred_element_type=F32).astype(BF16)
            lse_ref[rows, lanes] = jnp.broadcast_to(jnp.log(total) + top, (256, 64))


def attend_back_kernel(q_ref, k_ref, v_ref, d_ref, col_ref, row_ref, lse_ref, dq_ref, dk_ref, dv_ref, sk_ref, sv_ref):
    code_row = row_ref[...]
    turn = (((0,), (0,)), ((), ()))
    for head in range(2):
        lanes = slice(head * 64, head * 64 + 64)
        key = k_ref[:, lanes]
        value = v_ref[:, lanes]
        sk_ref[...] = jnp.zeros_like(sk_ref)
        sv_ref[...] = jnp.zeros_like(sv_ref)
        for block in range(4):
            rows = slice(block * 256, block * 256 + 256)
            query = q_ref[rows, lanes] * BF16(0.125)
            d_out = d_ref[rows, lanes]
            scores = scores_of(query, key, col_ref[rows, :], code_row)
            probs = jnp.exp(scores - lse_ref[rows, head * 64 : head * 64 + 1])
            d_probs = lax.dot_general(d_out, value, (((1,), (1,)), ((), ())), preferred_element_type=F32)
            delta = jnp.sum(probs * d_probs, axis=1, keepdims=True)
            d_scores = (probs * (d_probs - delta)).astype(BF16)
            dq_ref[rows, lanes] = (jnp.dot(d_scores, key, preferred_element_type=F32) * 0.125).astype(BF16)
            sk_ref[...] += lax.dot_general(d_scores, query, turn, preferred_element_type=F32)
            sv_ref[...] += lax.dot_general(probs.astype(BF16), d_out, turn, preferred_element_type=F32)
        dk_ref[:, lanes] = sk_ref[...].astype(BF16)
        dv_ref[:, lanes] = sv_ref[...].astype(BF16)


def two_heads(first):
    return pl.BlockSpec((1024, 128), lambda i: (0, first + i))


def whole(shape):
    return pl.BlockSpec(shape, lambda i: (0, 0))


def attend(qkv, code_col, code_row):
    return pl.pallas_call(
        attend_kernel,
        grid=(2,),
        in_specs=[two_heads(0), two_heads(2), two_heads(4), whole((1024, 1)), whole((1, 1024))],
        out_specs=[two_heads(0), two_heads(0)],
        out_shape=[jax.ShapeDtypeStruct((1024, 256), BF16), jax.ShapeDtypeStruct((1024, 256), F32)],
        compiler_params=pltpu.CompilerParams(vmem_limit_bytes=40 * 2**20),
        cost_estimate=pl.CostEstimate(flops=2 * 2 * 4 * 1024 * 1024 * 64 * 4, bytes_accessed=4 * 2**20, transcendentals=4 * 2**20),
        name="attend",
    )(qkv, qkv, qkv, code_col, code_row)


def attend_back(qkv, d_out, code_col, code_row, lse):
    return pl.pallas_call(
        attend_back_kernel,
        grid=(2,),
        in_specs=[two_heads(0), two_heads(2), two_heads(4), two_heads(0), whole((1024, 1)), whole((1, 1024)), two_heads(0)],
        out_specs=[two_heads(0)] * 3,
        out_shape=[jax.ShapeDtypeStruct((1024, 256), BF16)] * 3,
        scratch_shapes=[pltpu.VMEM((1024, 64), F32), pltpu.VMEM((1024, 64), F32)],
        compiler_params=pltpu.CompilerParams(vmem_limit_bytes=40 * 2**20),
        cost_estimate=pl.CostEstimate(flops=5 * 2 * 4 * 1024 * 1024 * 64 * 4, bytes_accessed=6 * 2**20, transcendentals=4 * 2**20),
        name="attend_back",
    )(qkv, qkv, qkv, d_out, code_col, code_row, lse)


def layer_norm(values_in, gain_vec, shift_vec):
    center = values_in - jnp.mean(values_in, axis=-1, keepdims=True)
    spread = jnp.mean(center * center, axis=-1, keepdims=True)
    return center * lax.rsqrt(spread + NORM_EPS) * gain_vec + shift_vec


def gelu_tanh(values_in):
    return jax.nn.gelu(values_in, approximate=True)


def lamb_step(weight, grad, first_mom, second_mom):
    new_first = BETA_ONE * first_mom + (1.0 - BETA_ONE) * grad
    new_second = BETA_TWO * second_mom + (1.0 - BETA_TWO) * grad * grad
    direction = (
        new_first
        / (1.0 - BETA_ONE**STEP_COUNT)
        / (jnp.sqrt(new_second / (1.0 - BETA_TWO**STEP_COUNT)) + ADAM_EPS)
        + WEIGHT_DECAY * weight
    )
    weight_norm = jnp.sqrt(jnp.sum(weight * weight))
    dir_norm = jnp.sqrt(jnp.sum(direction * direction))
    return direction * (weight_norm / jnp.maximum(dir_norm, 1.0))


def body(tokens, cotangent, doc_lengths, *params):
    shards, firsts, seconds = params[:7], params[7:14], params[14:]
    lowered = tuple(weight.astype(BF16) for weight in shards)
    dp_index = lax.axis_index("dp")
    z_at, y_at, core, x_at = dp_index // 8, dp_index // 2 % 4, dp_index % 2, lax.axis_index("group")

    with jax.named_scope("gather_tokens"):
        tok_all = jnp.concatenate([tokens] + [push(tokens, "x", -j) for j in (1, 2, 3)], axis=0)

    with jax.named_scope("gather_attn_in"):
        small = jnp.concatenate(
            [lowered[4], lowered[5], lowered[6].reshape(4, 8).T, jnp.zeros((8, 116), BF16)], axis=1
        )
        cols = lowered[0].reshape(8, 3, 4, 256)

        def slice_for(group):
            return jnp.concatenate([pick(cols, group, 2).reshape(8, 768), small], axis=1)

        parts = [slice_for(x_at)[None]] + [
            push(slice_for((x_at + 4 - j) % 4)[None], "x", -j) for j in (1, 2, 3)
        ]
        part = rolled(parts, x_at, 0)
        part = gather_small(part, "y", y_at, 0)
        part = gather_small(part, "z", z_at, 0)
        other = push(part, "core", 1)
        pair = jnp.stack([jnp.where(core == 0, part, other), jnp.where(core == 0, other, part)], axis=2)
        packed = pair.reshape(1024, 896)
        w_in = packed[:, :768]
        vectors = packed[:, 768:780].astype(F32).T
        gains, biases = vectors[:2], vectors[2:8]
        ffb = vectors[8:12].reshape(4, 128, 8).transpose(1, 0, 2).reshape(4096)

    with jax.named_scope("gather_ff_in"):
        part = gather_small(gather_small(lowered[2], "x", x_at, 0), "z", z_at, 0)
        w_up = gather_last(part, "y", y_at, core, jnp.zeros((4, 4, 2, 4, 8, 4096), BF16), 1, 0).reshape(1024, 4096)
    with jax.named_scope("gather_ff_out"):
        part = gather_small(gather_small(lowered[3], "x", x_at, 0), "y", y_at, 0)
        w_down = gather_last(part, "z", z_at, core, jnp.zeros((4, 4, 2, 4, 32, 1024), BF16), 0, 1).reshape(4096, 1024)
    with jax.named_scope("gather_attn_out"):
        part = gather_small(gather_small(lowered[1], "x", x_at, 0), "z", z_at, 0)
        w_out = gather_last(part, "y", y_at, core, jnp.zeros((4, 4, 2, 4, 8, 1024), BF16), 1, 0).reshape(1024, 1024)

    with jax.named_scope("attention"):
        order = (x_at + jnp.arange(4, dtype=jnp.int32)) % 4
        positions = (order[:, None] * 256 + jnp.arange(256, dtype=jnp.int32)[None]).reshape(1024)
        doc_ends = jnp.cumsum(doc_lengths[0])
        ids = jnp.sum((positions[:, None] >= doc_ends[None, :-1]).astype(jnp.int32), axis=1)
        code = (positions + 4096 * ids).astype(F32)
        code_col, code_row = code[:, None], code[None]
        own_cols = x_at * 256
        in_bias = jnp.concatenate(
            [
                lax.dynamic_slice_in_dim(biases[0], own_cols, 256),
                jnp.zeros((256,), F32),
                lax.dynamic_slice_in_dim(biases[1], own_cols, 256),
            ]
        )
        qkv = (jnp.dot(tok_all, w_in, preferred_element_type=F32) + in_bias).astype(BF16)
        out_all, lse = attend(qkv, code_col, code_row)
        blocks = out_all.reshape(4, 256, 256)
        context = rolled([blocks[0]] + [push(blocks[4 - j], "x", -j) for j in (1, 2, 3)], x_at, 1)

    with jax.named_scope("feed_forward"):
        attended = jnp.dot(context, w_out, preferred_element_type=F32) + biases[2]
        first, norm_one_pull = jax.vjp(layer_norm, tokens.astype(F32) + attended, gains[0], biases[3])
        first_low = first.astype(BF16)
        hidden = jnp.dot(first_low, w_up, preferred_element_type=F32) + ffb
        active, gelu_pull = jax.vjp(gelu_tanh, hidden)
        active_low = active.astype(BF16)
        branch = jnp.dot(active_low, w_down, preferred_element_type=F32) + biases[4]
        output, norm_two_pull = jax.vjp(layer_norm, first + branch, gains[1], biases[5])
        block_out = output.astype(BF16)

    with jax.named_scope("feed_forward_back"):
        d_two, d_gain_two, d_shift_two = norm_two_pull(cotangent.astype(F32))
        d_branch = d_two.astype(BF16)
        grad_down = jnp.einsum("tf,td->fd", active_low, d_branch, preferred_element_type=F32).astype(BF16)
        d_active = jnp.einsum("td,fd->tf", d_branch, w_down, preferred_element_type=F32)
        (d_hidden,) = gelu_pull(d_active)
        d_hidden_low = d_hidden.astype(BF16)
        grad_up = jnp.einsum("td,tf->df", first_low, d_hidden_low, preferred_element_type=F32).astype(BF16)
        d_first = d_two + jnp.einsum("tf,df->td", d_hidden_low, w_up, preferred_element_type=F32)
        d_one, d_gain_one, d_shift_one = norm_one_pull(d_first)
        d_attended = d_one.astype(BF16)
        grad_out = jnp.einsum("td,te->de", context, d_attended, preferred_element_type=F32).astype(BF16)
        d_context = jnp.einsum("te,de->td", d_attended, w_out, preferred_element_type=F32).astype(BF16)

    with jax.named_scope("scatter_ff_out"):
        value = core_sum(grad_down.reshape(4, 4, 2, 4, 32, 1024), core)
        value = scatter_two(value, "z", z_at, 0, BF16)
        value = scatter_direct(value, "y", y_at, 0, BF16)
        g_down = scatter_direct(value, "x", x_at, 0, F32)
    with jax.named_scope("scatter_ff_in"):
        value = core_sum(grad_up.reshape(4, 4, 2, 4, 8, 4096), core)
        value = scatter_two(value, "y", y_at, 1, BF16)
        value = scatter_direct(value, "z", z_at, 0, BF16)
        g_up = scatter_direct(value, "x", x_at, 0, F32)
    with jax.named_scope("scatter_attn_out"):
        value = core_sum(grad_out.reshape(4, 4, 2, 4, 8, 1024), core)
        value = scatter_direct(value, "x", x_at, 2, BF16)
        value = scatter_direct(value, "y", y_at, 1, BF16)
        g_out = scatter_direct(value, "z", z_at, 0, F32)

    with jax.named_scope("attention_back"):
        d_blocks = d_context.reshape(256, 4, 256)
        d_all = jnp.concatenate(
            [pick(d_blocks, x_at, 1)] + [push(pick(d_blocks, (x_at + 4 - j) % 4, 1), "x", -j) for j in (1, 2, 3)], axis=0
        )
        d_q, d_k, d_v = attend_back(qkv, d_all, code_col, code_row, lse)
        d_qkv = jnp.concatenate([d_q, d_k, d_v], axis=1)
        grad_in = jnp.einsum("td,te->de", tok_all, d_qkv, preferred_element_type=F32).astype(BF16)
        back = jnp.einsum("te,de->td", d_qkv, w_in, preferred_element_type=F32)

    with jax.named_scope("scatter_attn_in"):
        value = core_sum(grad_in.reshape(4, 4, 2, 4, 8, 768), core)
        value = scatter_direct(value, "y", y_at, 1, BF16)
        value = scatter_direct(value, "z", z_at, 0, F32)
        parts = [pick(value, x_at, 0)] + [push(pick(value, (x_at + 4 - j) % 4, 0), "x", -j) for j in (1, 2, 3)]
        g_in = rolled([p.reshape(8, 3, 1, 256) for p in parts], x_at, 2).reshape(8, 3072)

    with jax.named_scope("input_grad"):
        back_low = back.astype(BF16).reshape(4, 256, 1024)
        input_grad = d_one + back[:256]
        for j in (1, 3, 2):
            input_grad = input_grad + push(back_low[j], "x", j).astype(F32)

    with jax.named_scope("small_grads"):

        def at_heads(vec):
            return lax.dynamic_update_slice(jnp.zeros((1024,), F32), vec, (own_cols,))

        rows = jnp.stack(
            [
                d_gain_one,
                d_gain_two,
                at_heads(jnp.sum(d_q.astype(F32), axis=0)),
                at_heads(jnp.sum(d_v.astype(F32), axis=0)),
                jnp.sum(d_attended.astype(F32), axis=0),
                d_shift_one,
                jnp.sum(d_branch.astype(F32), axis=0),
                d_shift_two,
            ]
        )
        rows = jnp.concatenate([rows, jnp.sum(d_hidden_low.astype(F32), axis=0).reshape(4, 1024)], axis=0)
        rows = sum_all(rows, ("core", "y", "z", "x"))
        own = dp_index * 4 + x_at
        mine = lax.dynamic_slice(rows[:8], (0, own * 8), (8, 8)).T
        g_gains, g_biases = mine[:, :2], mine[:, 2:]
        g_ffb = lax.dynamic_slice(rows[8:], (own // 32, own % 32 * 32), (1, 32)).reshape(32)

    grads = (g_in, g_out, g_up.reshape(8, 4096), g_down.reshape(32, 1024), g_gains, g_biases, g_ffb)
    with jax.named_scope("norm"):
        squares = sum(jnp.sum(grad * grad) for grad in grads)
        squares = sum_all(squares.reshape(1, 1), ("core", "y", "z", "x"))[0, 0]
        factor = CLIP_NORM / jnp.maximum(jnp.sqrt(squares), CLIP_NORM)
    with jax.named_scope("lamb"):
        steps = tuple(
            lamb_step(weight, grad * factor, first_mom, second_mom)
            for weight, grad, first_mom, second_mom in zip(shards, grads, firsts, seconds)
        )
    return (block_out, input_grad, *grads, *steps)


def solution(mesh):
    rows, vector, docs = P(AXES, None), P(AXES), P("dp", None)
    leaves = (rows,) * 6 + (vector,)
    return jax.shard_map(
        body,
        mesh=mesh,
        in_specs=(rows, rows, docs) + leaves * 3,
        out_specs=(rows, rows) + leaves * 2,
        check_vma=False,
    )
```

time: 2770 us -> 572 us (0.21)
  waiting for transfers between devices: 2150 us -> 152 us
  blocking collectives: 378 us -> 0 us
  starting transfers between devices: 0.75 us -> 182 us
  matrix products: 114 us -> 43.5 us
  local copies, waits for them, and re-layouts: 35.8 us -> 81.3 us
  Pallas kernels: 0 us -> 30.8 us
    reduce_scatter x5 -> x0, waiting for transfers between devices: 1720 us -> none  [the longest x1 669 us: body(): lax.psum_scatter(partial_grads[3], ('dp', 'group'), scatter_dimension=0,...]
    unnamed x13 -> x0, waiting for transfers between devices: 302 us -> none
    ppermute x0 -> x129, starting transfers between devices: none -> 182 us  [push(): return lax.ppermute(value, AXES, pair_list(axis, shift))]
    ppermute x0 -> x129, waiting for transfers between devices: none -> 152 us  [push(): return lax.ppermute(value, AXES, pair_list(axis, shift))]
    psum x1 -> x0, blocking collectives: 141 us -> none  [body(): all_squares = lax.psum(local_squares, ('dp', 'group'))]
    unnamed x2 -> x0, blocking collectives: 131 us -> none
    all_gather x6 -> x0, waiting for transfers between devices: 128 us -> none  [the longest x4 128 us: body(): lax.all_gather(shortened(lowered), ('dp', 'group'), axis=0, tiled=True)]
    all_gather x2 -> x0, blocking collectives: 106 us -> none  [body(): lax.all_gather(shortened(lowered), ('dp', 'group'), axis=0, tiled=True)]
  transfers between devices with their start and end apart: 12 -> 129, of which waited for: 8 -> 57; matrix products, arithmetic and copies ran while one was open for 5% -> 21% of each run, Pallas kernels for 0% -> 5%
where the time goes in v1:
time: 572 us; the launch traced here: 562 us
  starting transfers between devices  182 us (32%)
  waiting for transfers between devices  152 us (27%)
  local copies, waits for them, and re-layouts  81.3 us (14%)
  other arithmetic  48.9 us (9%)
  matrix products  43.5 us (8%)
  Pallas kernels  30.8 us (5%)
  between operations  23.7 us (4%)
    ppermute x129, starting transfers between devices, push(): return lax.ppermute(value, AXES, pair_list(axis, shift))  182 us
    ppermute x129, waiting for transfers between devices, push(): return lax.ppermute(value, AXES, pair_list(axis, shift))  152 us
    dynamic_update_slice x30, local copies, waits for them, and re-layouts, put(): buf = lax.dynamic_update_slice(buf, data, tuple(at))  23 us
    pallas_call x1, Pallas kernels, attend_back(): pl.pallas_call(attend_back_kernel, grid=(2,), in_specs=[two_heads(0), two...  18.4 us
    unnamed x230, local copies, waits for them, and re-layouts  18.3 us
    dynamic_slice x6, local copies, waits for them, and re-layouts, pick(): return lax.dynamic_index_in_dim(value, index, dim, keepdims=False)  15.3 us
    pallas_call x1, Pallas kernels, attend(): pl.pallas_call(attend_kernel, grid=(2,), in_specs=[two_heads(0), two_head...  12.4 us
  transfers between devices with their start and end apart: 129, of which 57 were waited for; matrix products, arithmetic and copies ran while one was open for 21% of the time, Pallas kernels for 5%

profile of v1, /device:TPU:34, one launch (start us, length us, event | category | flops | bytes accessed | tf_op | source)
XLA Modules:
  0.0 562.0 jit_solution(12695818406347853066)
XLA Ops:
  24.1 2.6 collective-permute-start.5
  30.5 2.8 collective-permute-start.18
  33.7 3.2 collective-permute-start.31
  44.2 3.1 collective-permute-start.6
  49.5 3.6 collective-permute-done.7
  53.1 3.0 collective-permute-start.20
  60.4 4.1 collective-permute-start.10
  65.7 3.3 collective-permute-start.11
  69.0 3.3 collective-permute-done.10
  73.7 3.7 collective-permute-done.11
  77.4 6.4 %collective-permute-start.34 = (bf16[1,4,8,4096]{3,2,1,0:T(8,128)(2,1)S(1)}, bf16[1,4,8,4096]{3,2,1,0:T(8,128)(2,1)S(1)}, u32[]{:S(2)}, u32[]{:S(2)}) collective-permute-start(bf16[1,4,8,4096]{3,2,1,0:T(8,128)(2,1)S(1)} %get-tuple-element.141), channel_id=1, source_target_pairs={{0,96},{1,97},{2,98},{3,99},{4,100},{5,101},{6,102},{7,103},{8,104... | collective-permute-start | bytes 786440 | tf_op jit(solution)/shard_map/gather_ff_in/ppermute | solution.py:35
  84.0 3.7 collective-permute-done.34
  87.6 3.2 collective-permute-start.35
  90.9 4.6 collective-permute-done.35
  96.6 6.5 %collective-permute-done.51 = bf16[1,4,32,1024]{3,2,1,0:T(8,128)(2,1)S(1)} collective-permute-done((bf16[1,4,32,1024]{3,2,1,0:T(8,128)(2,1)S(1)}, bf16[1,4,32,1024]{3,2,1,0:T(8,128)(2,1)S(1)}, u32[]{:S(2)}, u32[]{:S(2)}) %collective-permute-start.51) | collective-permute-done | bytes 262176 | tf_op jit(solution)/shard_map/gather_ff_out/ppermute | solution.py:35
  107.6 3.3 copy-done.7
  113.2 2.6 collective-permute-start.2
  116.8 2.6 collective-permute-start.53
  119.3 3.2 collective-permute-done.2
  122.5 2.6 collective-permute-start.27
  127.7 6.5 %collective-permute-done.29 = bf16[2,4,8,1024]{3,2,1,0:T(8,128)(2,1)S(1)} collective-permute-done((bf16[2,4,8,1024]{3,2,1,0:T(8,128)(2,1)S(1)}, bf16[2,4,8,1024]{3,2,1,0:T(8,128)(2,1)S(1)}, u32[]{:S(2)}, u32[]{:S(2)}) %collective-permute-start.29) | collective-permute-done | bytes 131104 | tf_op jit(solution)/shard_map/gather_attn_out/ppermute | solution.py:35
  134.2 3.2 collective-permute-start.55
  145.0 12.4 %attend.1 = (bf16[1024,256]{1,0:T(8,128)(2,1)S(1)}, f32[1024,256]{1,0:T(8,128)S(1)}) custom-call(bf16[1024,768]{1,0:T(8,128)(2,1)S(1)} %add_convert_fusion.q_ref.k_ref.v_ref, bf16[1024,768]{1,0:T(8,128)(2,1)S(1)} %add_convert_fusion.q_ref.k_ref.v_ref, bf16[1024,768]{1,0:T(8,128)(2,1)S(1)} %add_convert_fusion.q_ref.k_ref.v_ref, ...), custom_call_target="tpu_custom_call" | custom-call | flops 4294967296 | bytes 4194304 | tf_op jit(solution)/shard_map/attention/attend/pallas_call | solution.py:169
  165.7 2.5 collective-permute-start.15
  177.2 2.7 fusion.122
  187.0 10.3 %collective-permute-done.38 = bf16[4,4,8,4096]{3,2,1,0:T(8,128)(2,1)S(1)} collective-permute-done((bf16[4,4,8,4096]{3,2,1,0:T(8,128)(2,1)}, bf16[4,4,8,4096]{3,2,1,0:T(8,128)(2,1)S(1)}, u32[]{:S(2)}, u32[]{:S(2)}) %collective-permute-start.38) | collective-permute-done | bytes 1048608 | tf_op jit(solution)/shard_map/gather_ff_in/ppermute | solution.py:35
  201.8 5.0 collective-permute-done.40
  212.8 7.2 %collective-permute-done.42 = bf16[2,4,8,4096]{3,2,1,0:T(8,128)(2,1)S(1)} collective-permute-done((bf16[2,4,8,4096]{3,2,1,0:T(8,128)(2,1)S(1)}, bf16[2,4,8,4096]{3,2,1,0:T(8,128)(2,1)S(1)}, u32[]{:S(2)}, u32[]{:S(2)}) %collective-permute-start.42) | collective-permute-done | bytes 524320 | tf_op jit(solution)/shard_map/gather_ff_in/ppermute | solution.py:35
  232.3 6.4 %convolution_add_fusion = f32[256,4096]{1,0:T(8,128)S(1)} fusion(bf16[1024,4096]{1,0:T(8,128)(2,1)} %bitcast.399, f32[4096]{0:T(1024)S(1)} %add.917, f32[256,1024]{1,0:T(8,128)S(1)} %get-tuple-element.242, f32[1024]{0:T(1024)S(1)} %get-tuple-element.99, f32[1024]{0:T(1024)S(1)} %get-tuple-element.100, f32[256]{0:T(256)S(1)} %fusion.102, ...), kind=kOutput, calls=%fused_computation.8 | convolution fusion | flops 2149842944 | bytes 13658112 | tf_op jit(solution)/shard_map/feed_forward/dot_general | solution.py:285
  238.8 3.0 fusion.123
  244.6 6.0 %convert_reduce_fusion = (f32[4096]{0:T(1024)}, bf16[256,4096]{1,0:T(8,128)(2,1)S(1)}) fusion(f32[256,4096]{1,0:T(8,128)S(1)} %convolution_add_fusion, bf16[256,1024]{1,0:T(8,128)(2,1)S(1)} %get-tuple-element.131, bf16[4096,1024]{1,0:T(8,128)(2,1)S(1)} %bitcast.398), kind=kOutput, calls=%fused_computation.18 | convolution fusion | flops 2170548224 | bytes 15220736 | tf_op jit(solution)/shard_map/feed_forward_back/td,fd->tf/dot_general | solution.py:296
  250.6 3.3 multiply_reduce_fusion
  259.1 5.9 %convolution_convert_fusion.1 = bf16[1024,4096]{1,0:T(8,128)(2,1)} fusion(bf16[256,4096]{1,0:T(8,128)(2,1)S(1)} %get-tuple-element.129, f32[256,1024]{1,0:T(8,128)S(1)} %get-tuple-element.242, f32[1024]{0:T(1024)S(1)} %get-tuple-element.99, f32[1024]{0:T(1024)S(1)} %get-tuple-element.100, f32[256]{0:T(256)S(1)} %fusion.102, f32[256]{0:T(256)S(1)} %broadcast_multiply_fusion.8), kind=kOutput, calls=%fused_computation.5 | convolution fusion | flops 2152988672 | bytes 11544576 | tf_op jit(solution)/shard_map/feed_forward_back/td,tf->df/dot_general | solution.py:299
  265.0 5.5 convolution_convert_fusion
  272.8 2.9 constant_dynamic-slice_fusion.17
  277.6 2.6 collective-permute-start.61
  280.2 2.8 constant_dynamic-slice_fusion.8
  284.1 3.8 constant_dynamic-slice_fusion.2
  287.9 4.6 copy.230
  293.9 5.1 dynamic-slice_bitcast_fusion
  300.1 18.4 %attend_back.1 = (bf16[1024,256]{1,0:T(8,128)(2,1)S(1)}, bf16[1024,256]{1,0:T(8,128)(2,1)S(1)}, bf16[1024,256]{1,0:T(8,128)(2,1)S(1)}) custom-call(bf16[1024,768]{1,0:T(8,128)(2,1)S(1)} %add_convert_fusion.q_ref.k_ref.v_ref, bf16[1024,768]{1,0:T(8,128)(2,1)S(1)} %add_convert_fusion.q_ref.k_ref.v_ref, ...), custom_call_target="tpu_custom_call" | custom-call | flops 10737418240 | bytes 6291456 | tf_op jit(solution)/shard_map/attention_back/attend_back/pallas_call | solution.py:182
  320.0 3.5 convolution_convert_fusion.3
  323.9 2.7 collective-permute-start.111
  340.8 2.5 collective-permute-start.116
  343.4 7.4 %collective-permute-done.118 = f32[12,1024]{1,0:T(8,128)S(1)} collective-permute-done((f32[12,1024]{1,0:T(8,128)S(1)}, f32[12,1024]{1,0:T(8,128)S(1)}, u32[]{:S(2)}, u32[]{:S(2)}) %collective-permute-start.118) | collective-permute-done | bytes 49184 | tf_op jit(solution)/shard_map/small_grads/ppermute | solution.py:35
  356.4 8.2 %collective-permute-done.65 = bf16[256,1024]{1,0:T(8,128)(2,1)S(1)} collective-permute-done((bf16[256,1024]{1,0:T(8,128)(2,1)S(1)}, bf16[256,1024]{1,0:T(8,128)(2,1)S(1)}, u32[]{:S(2)}, u32[]{:S(2)}) %collective-permute-start.65) | collective-permute-done | bytes 524320 | tf_op jit(solution)/shard_map/input_grad/ppermute | solution.py:35
  370.1 6.2 %collective-permute-done.70 = bf16[4,4,8,768]{3,2,1,0:T(8,128)(2,1)S(1)} collective-permute-done((bf16[4,4,8,768]{3,2,1,0:T(8,128)(2,1)S(1)}, bf16[4,4,8,768]{3,2,1,0:T(8,128)(2,1)S(1)}, u32[]{:S(2)}, u32[]{:S(2)}) %collective-permute-start.70) | collective-permute-done | bytes 196640 | tf_op jit(solution)/shard_map/scatter_attn_in/ppermute | solution.py:35
  379.6 3.0 collective-permute-start.73
  389.7 2.5 collective-permute-start.76
  398.3 4.5 collective-permute-done.80
  402.8 2.7 collective-permute-done.79
  408.7 3.7 collective-permute-done.83
  417.1 3.6 fusion.1
  421.9 3.2 collective-permute-start.90
  425.2 3.7 fusion
  437.5 3.1 collective-permute-start.91
  443.0 2.5 collective-permute-done.85
  454.0 2.5 collective-permute-start.102
  456.7 3.4 collective-permute-done.91
  460.1 4.4 collective-permute-done.89
  470.2 9.7 %collective-permute-done.102 = bf16[4,4,32,1024]{3,2,1,0:T(8,128)(2,1)S(1)} collective-permute-done((bf16[4,4,32,1024]{3,2,1,0:T(8,128)(2,1)S(1)}, bf16[4,4,32,1024]{3,2,1,0:T(8,128)(2,1)S(1)}, u32[]{:S(2)}, u32[]{:S(2)}) %collective-permute-start.102) | collective-permute-done | bytes 1048608 | tf_op jit(solution)/shard_map/scatter_ff_out/ppermute | solution.py:35
  508.3 5.2 collective-permute-start.121
  519.3 8.8 %collective-permute-start.124 = (f32[1,1]{1,0:T(1,128)}, f32[1,1]{1,0:T(1,128)}, u32[]{:S(2)}, u32[]{:S(2)}) collective-permute-start(f32[1,1]{1,0:T(1,128)} %add.1008), channel_id=1, source_target_pairs={{0,64},{1,65},{2,66},{3,67},{4,68},{5,69},{6,70},{7,71},{8,72},{9,... | collective-permute-start | bytes 20 | tf_op jit(solution)/shard_map/norm/ppermute | solution.py:35
  534.7 5.6 collective-permute-start.127
  (623 shorter events, 243.9 us)
Async XLA Ops:
  1.6 38.6 %collective-permute-start.46 = (bf16[1,32,1024]{2,1,0:T(8,128)(2,1)S(1)}, bf16[1,32,1024]{2,1,0:T(8,128)(2,1)S(1)}, u32[]{:S(2)}, u32[]{:S(2)}) collective-permute-start(bf16[1,32,1024]{2,1,0:T(8,128)(2,1)S(1)} %get-tuple-element.159), channel_id=1, source_target_pairs={{0,3},{1,0},{2,1},{3,2},{4,7},{5,4},{6,5},{7,6},{8,11},{9,8},{10,9... | collective-permute-start | bytes 196616 | tf_op jit(solution)/shard_map/gather_ff_out/ppermute | solution.py:35
  2.2 39.9 %collective-permute-start.47 = (bf16[1,32,1024]{2,1,0:T(8,128)(2,1)S(1)}, bf16[1,32,1024]{2,1,0:T(8,128)(2,1)S(1)}, u32[]{:S(2)}, u32[]{:S(2)}) collective-permute-start(bf16[1,32,1024]{2,1,0:T(8,128)(2,1)S(1)} %get-tuple-element.159), channel_id=1, source_target_pairs={{0,2},{1,3},{2,0},{3,1},{4,6},{5,7},{6,4},{7,5},{8,10},{9,11},{10,... | collective-permute-start | bytes 196616 | tf_op jit(solution)/shard_map/gather_ff_out/ppermute | solution.py:35
  4.6 39.6 %collective-permute-start.48 = (bf16[1,32,1024]{2,1,0:T(8,128)(2,1)S(1)}, bf16[1,32,1024]{2,1,0:T(8,128)(2,1)S(1)}, u32[]{:S(2)}, u32[]{:S(2)}) collective-permute-start(bf16[1,32,1024]{2,1,0:T(8,128)(2,1)S(1)} %get-tuple-element.159), channel_id=1, source_target_pairs={{0,1},{1,2},{2,3},{3,0},{4,5},{5,6},{6,7},{7,4},{8,9},{9,10},{10,1... | collective-permute-start | bytes 196616 | tf_op jit(solution)/shard_map/gather_ff_out/ppermute | solution.py:35
  12.5 11.6 %collective-permute-start.3 = (bf16[1,8,896]{2,1,0:T(8,128)(2,1)S(1)}, bf16[1,8,896]{2,1,0:T(8,128)(2,1)S(1)}, u32[]{:S(2)}, u32[]{:S(2)}) collective-permute-start(bf16[1,8,896]{2,1,0:T(8,128)(2,1)S(1)} %bitcast.439), channel_id=1, source_target_pairs={{0,3},{1,0},{2,1},{3,2},{4,7},{5,4},{6,5},{7,6},{8,11},{9,8},{10,9... | collective-permute-start | bytes 43016 | tf_op jit(solution)/shard_map/gather_attn_in/ppermute | solution.py:35
  12.8 13.9 %collective-permute-start.4 = (bf16[1,8,896]{2,1,0:T(8,128)(2,1)S(1)}, bf16[1,8,896]{2,1,0:T(8,128)(2,1)S(1)}, u32[]{:S(2)}, u32[]{:S(2)}) collective-permute-start(bf16[1,8,896]{2,1,0:T(8,128)(2,1)S(1)} %bitcast.438), channel_id=1, source_target_pairs={{0,2},{1,3},{2,0},{3,1},{4,6},{5,7},{6,4},{7,5},{8,10},{9,11},{10,... | collective-permute-start | bytes 43016 | tf_op jit(solution)/shard_map/gather_attn_in/ppermute | solution.py:35
  37.0 10.4 %collective-permute-start.32 = (bf16[1,8,4096]{2,1,0:T(8,128)(2,1)S(1)}, bf16[1,8,4096]{2,1,0:T(8,128)(2,1)S(1)}, u32[]{:S(2)}, u32[]{:S(2)}) collective-permute-start(bf16[1,8,4096]{2,1,0:T(8,128)(2,1)S(1)} %get-tuple-element.143), channel_id=1, source_target_pairs={{0,2},{1,3},{2,0},{3,1},{4,6},{5,7},{6,4},{7,5},{8,10},{9,11},{10,... | collective-permute-start | bytes 196616 | tf_op jit(solution)/shard_map/gather_ff_in/ppermute | solution.py:35
  40.2 76.4 %collective-permute-start = (bf16[256,1024]{1,0:T(8,128)(2,1)S(1)}, bf16[256,1024]{1,0:T(8,128)(2,1)S(1)}, u32[]{:S(2)}, u32[]{:S(2)}) collective-permute-start(bf16[256,1024]{1,0:T(8,128)(2,1)S(1)} %copy-done.17), channel_id=1, source_target_pairs={{0,3},{1,0},{2,1},{3,2},{4,7},{5,4},{6,5},{7,6},{8,11},{9,8},{10,9... | collective-permute-start | bytes 1572872 | tf_op jit(solution)/shard_map/gather_tokens/ppermute | solution.py:35
  42.1 74.7 %collective-permute-start.1 = (bf16[256,1024]{1,0:T(8,128)(2,1)S(1)}, bf16[256,1024]{1,0:T(8,128)(2,1)S(1)}, u32[]{:S(2)}, u32[]{:S(2)}) collective-permute-start(bf16[256,1024]{1,0:T(8,128)(2,1)S(1)} %copy-done.17), channel_id=1, source_target_pairs={{0,2},{1,3},{2,0},{3,1},{4,6},{5,7},{6,4},{7,5},{8,10},{9,11},{10,... | collective-permute-start | bytes 1572872 | tf_op jit(solution)/shard_map/gather_tokens/ppermute | solution.py:35
  56.3 39.2 %collective-permute-start.49 = (bf16[1,4,32,1024]{3,2,1,0:T(8,128)(2,1)S(1)}, bf16[1,4,32,1024]{3,2,1,0:T(8,128)(2,1)S(1)}, u32[]{:S(2)}, u32[]{:S(2)}) collective-permute-start(bf16[1,4,32,1024]{3,2,1,0:T(8,128)(2,1)S(1)} %get-tuple-element.157), channel_id=1, source_target_pairs={{0,24},{1,25},{2,26},{3,27},{4,28},{5,29},{6,30},{7,31},{8,0},{9,1... | collective-permute-start | bytes 786440 | tf_op jit(solution)/shard_map/gather_ff_out/ppermute | solution.py:35
  60.4 11.9 %collective-permute-start.10 = (bf16[1,4,4,8,896]{4,3,2,1,0:T(8,128)(2,1)S(1)}, bf16[1,4,4,8,896]{4,3,2,1,0:T(8,128)(2,1)S(1)}, u32[]{:S(2)}, u32[]{:S(2)}) collective-permute-start(bf16[1,4,4,8,896]{4,3,2,1,0:T(8,128)(2,1)S(1)} %get-tuple-element.145), channel_id=1, source_target_pairs={{0,64},{1,65},{2,66},{3,67},{4,68},{5,69},{6,70},{7,71},{8,72},{9,... | collective-permute-start | bytes 688136 | tf_op jit(solution)/shard_map/gather_attn_in/ppermute | solution.py:35
  65.7 11.7 %collective-permute-start.11 = (bf16[1,4,4,8,896]{4,3,2,1,0:T(8,128)(2,1)S(1)}, bf16[1,4,4,8,896]{4,3,2,1,0:T(8,128)(2,1)S(1)}, u32[]{:S(2)}, u32[]{:S(2)}) collective-permute-start(bf16[1,4,4,8,896]{4,3,2,1,0:T(8,128)(2,1)S(1)} %get-tuple-element.145), channel_id=1, source_target_pairs={{0,32},{1,33},{2,34},{3,35},{4,36},{5,37},{6,38},{7,39},{8,40},{9,... | collective-permute-start | bytes 688136 | tf_op jit(solution)/shard_map/gather_attn_in/ppermute | solution.py:35
  72.3 24.1 %collective-permute-start.50 = (bf16[1,4,32,1024]{3,2,1,0:T(8,128)(2,1)S(1)}, bf16[1,4,32,1024]{3,2,1,0:T(8,128)(2,1)S(1)}, u32[]{:S(2)}, u32[]{:S(2)}) collective-permute-start(bf16[1,4,32,1024]{3,2,1,0:T(8,128)(2,1)S(1)} %get-tuple-element.157), channel_id=1, source_target_pairs={{0,16},{1,17},{2,18},{3,19},{4,20},{5,21},{6,22},{7,23},{8,24},{9,... | collective-permute-start | bytes 786440 | tf_op jit(solution)/shard_map/gather_ff_out/ppermute | solution.py:35
  77.4 10.2 %collective-permute-start.34 = (bf16[1,4,8,4096]{3,2,1,0:T(8,128)(2,1)S(1)}, bf16[1,4,8,4096]{3,2,1,0:T(8,128)(2,1)S(1)}, u32[]{:S(2)}, u32[]{:S(2)}) collective-permute-start(bf16[1,4,8,4096]{3,2,1,0:T(8,128)(2,1)S(1)} %get-tuple-element.141), channel_id=1, source_target_pairs={{0,96},{1,97},{2,98},{3,99},{4,100},{5,101},{6,102},{7,103},{8,104... | collective-permute-start | bytes 786440 | tf_op jit(solution)/shard_map/gather_ff_in/ppermute | solution.py:35
  96.4 16.8 %collective-permute-start.22 = (bf16[4,4,8,1024]{3,2,1,0:T(8,128)(2,1)S(1)}, bf16[4,4,8,1024]{3,2,1,0:T(8,128)(2,1)S(1)}, u32[]{:S(2)}, u32[]{:S(2)}) collective-permute-start(bf16[4,4,8,1024]{3,2,1,0:T(8,128)(2,1)S(1)} %get-tuple-element.149), channel_id=1, source_target_pairs={{0,4},{1,5},{2,6},{3,7},{4,0},{5,1},{6,2},{7,3},{8,12},{9,13},{10,... | collective-permute-start | bytes 786440 | tf_op jit(solution)/shard_map/gather_attn_out/ppermute | solution.py:35
  103.1 12.7 %collective-permute-start.23 = (bf16[4,4,8,1024]{3,2,1,0:T(8,128)(2,1)S(1)}, bf16[4,4,8,1024]{3,2,1,0:T(8,128)(2,1)S(1)}, u32[]{:S(2)}, u32[]{:S(2)}) collective-permute-start(bf16[4,4,8,1024]{3,2,1,0:T(8,128)(2,1)S(1)} %get-tuple-element.149), channel_id=1, source_target_pairs={{0,24},{1,25},{2,26},{3,27},{4,28},{5,29},{6,30},{7,31},{8,0},{9,1... | collective-permute-start | bytes 786440 | tf_op jit(solution)/shard_map/gather_attn_out/ppermute | solution.py:35
  103.2 12.8 %collective-permute-start.25 = (bf16[4,4,8,1024]{3,2,1,0:T(8,128)(2,1)S(1)}, bf16[4,4,8,1024]{3,2,1,0:T(8,128)(2,1)S(1)}, u32[]{:S(2)}, u32[]{:S(2)}) collective-permute-start(bf16[4,4,8,1024]{3,2,1,0:T(8,128)(2,1)S(1)} %get-tuple-element.149), channel_id=1, source_target_pairs={{0,8},{1,9},{2,10},{3,11},{4,12},{5,13},{6,14},{7,15},{8,16},{9,17... | collective-permute-start | bytes 786440 | tf_op jit(solution)/shard_map/gather_attn_out/ppermute | solution.py:35
  115.8 23.4 %collective-permute-start.12 = (bf16[4,4,4,8,896]{4,3,2,1,0:T(8,128)(2,1)S(1)}, bf16[4,4,4,8,896]{4,3,2,1,0:T(8,128)(2,1)S(1)}, u32[]{:S(2)}, u32[]{:S(2)}) collective-permute-start(bf16[4,4,4,8,896]{4,3,2,1,0:T(8,128)(2,1)S(1)} %constant_dynamic-slice_fusion.21), channel_id=1, source_target_pairs={{0,4},{1,5},{2,6},{3,7},{4,0},{5,1},{6,2},{7,3},{8,12},{9,13},{10,... | collective-permute-start | bytes 2752520 | tf_op jit(solution)/shard_map/gather_attn_in/ppermute | solution.py:35
  116.0 66.6 %collective-permute-start.52 = (bf16[4,4,32,1024]{3,2,1,0:T(8,128)(2,1)}, bf16[4,4,32,1024]{3,2,1,0:T(8,128)(2,1)}, u32[]{:S(2)}, u32[]{:S(2)}) collective-permute-start(bf16[4,4,32,1024]{3,2,1,0:T(8,128)(2,1)} %get-tuple-element.155), channel_id=1, source_target_pairs={{0,4},{1,5},{2,6},{3,7},{4,0},{5,1},{6,2},{7,3},{8,12},{9,13},{10,... | collective-permute-start | bytes 3145736 | tf_op jit(solution)/shard_map/gather_ff_out/ppermute | solution.py:35
  116.8 63.4 %collective-permute-start.53 = (bf16[4,4,32,1024]{3,2,1,0:T(8,128)(2,1)}, bf16[4,4,32,1024]{3,2,1,0:T(8,128)(2,1)}, u32[]{:S(2)}, u32[]{:S(2)}) collective-permute-start(bf16[4,4,32,1024]{3,2,1,0:T(8,128)(2,1)} %get-tuple-element.155), channel_id=1, source_target_pairs={{0,96},{1,97},{2,98},{3,99},{4,100},{5,101},{6,102},{7,103},{8,104... | collective-permute-start | bytes 3145736 | tf_op jit(solution)/shard_map/gather_ff_out/ppermute | solution.py:35
  127.6 9.8 %collective-permute-start.28 = (bf16[2,4,8,1024]{3,2,1,0:T(8,128)(2,1)S(1)}, bf16[2,4,8,1024]{3,2,1,0:T(8,128)(2,1)S(1)}, u32[]{:S(2)}, u32[]{:S(2)}) collective-permute-start(bf16[2,4,8,1024]{3,2,1,0:T(8,128)(2,1)S(1)} %collective-permute-done.27), channel_id=1, source_target_pairs={{0,4},{1,5},{2,6},{3,7},{4,0},{5,1},{6,2},{7,3},{8,12},{9,13},{10,... | collective-permute-start | bytes 393224 | tf_op jit(solution)/shard_map/gather_attn_out/ppermute | solution.py:35
  134.2 47.2 %collective-permute-start.55 = (bf16[4,4,32,1024]{3,2,1,0:T(8,128)(2,1)}, bf16[4,4,32,1024]{3,2,1,0:T(8,128)(2,1)}, u32[]{:S(2)}, u32[]{:S(2)}) collective-permute-start(bf16[4,4,32,1024]{3,2,1,0:T(8,128)(2,1)} %get-tuple-element.155), channel_id=1, source_target_pairs={{0,32},{1,33},{2,34},{3,35},{4,36},{5,37},{6,38},{7,39},{8,40},{9,... | collective-permute-start | bytes 3145736 | tf_op jit(solution)/shard_map/gather_ff_out/ppermute | solution.py:35
  169.7 17.2 %collective-permute-start.37 = (bf16[4,4,8,4096]{3,2,1,0:T(8,128)(2,1)}, bf16[4,4,8,4096]{3,2,1,0:T(8,128)(2,1)S(1)}, u32[]{:S(2)}, u32[]{:S(2)}) collective-permute-start(bf16[4,4,8,4096]{3,2,1,0:T(8,128)(2,1)} %get-tuple-element.139), channel_id=1, source_target_pairs={{0,4},{1,5},{2,6},{3,7},{4,0},{5,1},{6,2},{7,3},{8,12},{9,13},{10,... | collective-permute-start | bytes 3145736 | tf_op jit(solution)/shard_map/gather_ff_in/ppermute | solution.py:35
  171.3 25.9 %collective-permute-start.38 = (bf16[4,4,8,4096]{3,2,1,0:T(8,128)(2,1)}, bf16[4,4,8,4096]{3,2,1,0:T(8,128)(2,1)S(1)}, u32[]{:S(2)}, u32[]{:S(2)}) collective-permute-start(bf16[4,4,8,4096]{3,2,1,0:T(8,128)(2,1)} %get-tuple-element.139), channel_id=1, source_target_pairs={{0,24},{1,25},{2,26},{3,27},{4,28},{5,29},{6,30},{7,31},{8,0},{9,1... | collective-permute-start | bytes 3145736 | tf_op jit(solution)/shard_map/gather_ff_in/ppermute | solution.py:35
  180.2 26.6 %collective-permute-start.40 = (bf16[4,4,8,4096]{3,2,1,0:T(8,128)(2,1)S(1)}, bf16[4,4,8,4096]{3,2,1,0:T(8,128)(2,1)S(1)}, u32[]{:S(2)}, u32[]{:S(2)}) collective-permute-start(bf16[4,4,8,4096]{3,2,1,0:T(8,128)(2,1)S(1)} %copy-done.15), channel_id=1, source_target_pairs={{0,8},{1,9},{2,10},{3,11},{4,12},{5,13},{6,14},{7,15},{8,16},{9,17... | collective-permute-start | bytes 3145736 | tf_op jit(solution)/shard_map/gather_ff_in/ppermute | solution.py:35
  181.4 30.8 %collective-permute-start.57 = (bf16[2,4,32,1024]{3,2,1,0:T(8,128)(2,1)S(1)}, bf16[2,4,32,1024]{3,2,1,0:T(8,128)(2,1)S(1)}, u32[]{:S(2)}, u32[]{:S(2)}) collective-permute-start(bf16[2,4,32,1024]{3,2,1,0:T(8,128)(2,1)S(1)} %slice.234), channel_id=1, source_target_pairs={{0,96},{1,97},{2,98},{3,99},{4,100},{5,101},{6,102},{7,103},{8,104... | collective-permute-start | bytes 1572872 | tf_op jit(solution)/shard_map/gather_ff_out/ppermute | solution.py:35
  182.6 30.1 %collective-permute-start.59 = (bf16[2,4,32,1024]{3,2,1,0:T(8,128)(2,1)S(1)}, bf16[2,4,32,1024]{3,2,1,0:T(8,128)(2,1)S(1)}, u32[]{:S(2)}, u32[]{:S(2)}) collective-permute-start(bf16[2,4,32,1024]{3,2,1,0:T(8,128)(2,1)S(1)} %slice.235), channel_id=1, source_target_pairs={{0,32},{1,33},{2,34},{3,35},{4,36},{5,37},{6,38},{7,39},{8,40},{9,... | collective-permute-start | bytes 1572872 | tf_op jit(solution)/shard_map/gather_ff_out/ppermute | solution.py:35
  187.0 23.1 %collective-permute-start.54 = (bf16[4,4,32,1024]{3,2,1,0:T(8,128)(2,1)}, bf16[4,4,32,1024]{3,2,1,0:T(8,128)(2,1)S(1)}, u32[]{:S(2)}, u32[]{:S(2)}) collective-permute-start(bf16[4,4,32,1024]{3,2,1,0:T(8,128)(2,1)} %collective-permute-done.53), channel_id=1, source_target_pairs={{0,4},{1,5},{2,6},{3,7},{4,0},{5,1},{6,2},{7,3},{8,12},{9,13},{10,... | collective-permute-start | bytes 3145736 | tf_op jit(solution)/shard_map/gather_ff_out/ppermute | solution.py:35
  206.8 13.2 %collective-permute-start.42 = (bf16[2,4,8,4096]{3,2,1,0:T(8,128)(2,1)S(1)}, bf16[2,4,8,4096]{3,2,1,0:T(8,128)(2,1)S(1)}, u32[]{:S(2)}, u32[]{:S(2)}) collective-permute-start(bf16[2,4,8,4096]{3,2,1,0:T(8,128)(2,1)S(1)} %slice.231), channel_id=1, source_target_pairs={{0,24},{1,25},{2,26},{3,27},{4,28},{5,29},{6,30},{7,31},{8,0},{9,1... | collective-permute-start | bytes 1572872 | tf_op jit(solution)/shard_map/gather_ff_in/ppermute | solution.py:35
  206.8 14.5 %collective-permute-start.44 = (bf16[2,4,8,4096]{3,2,1,0:T(8,128)(2,1)S(1)}, bf16[2,4,8,4096]{3,2,1,0:T(8,128)(2,1)S(1)}, u32[]{:S(2)}, u32[]{:S(2)}) collective-permute-start(bf16[2,4,8,4096]{3,2,1,0:T(8,128)(2,1)S(1)} %slice.232), channel_id=1, source_target_pairs={{0,8},{1,9},{2,10},{3,11},{4,12},{5,13},{6,14},{7,15},{8,16},{9,17... | collective-permute-start | bytes 1572872 | tf_op jit(solution)/shard_map/gather_ff_in/ppermute | solution.py:35
  210.0 11.3 %collective-permute-start.41 = (bf16[4,4,8,4096]{3,2,1,0:T(8,128)(2,1)S(1)}, bf16[4,4,8,4096]{3,2,1,0:T(8,128)(2,1)S(1)}, u32[]{:S(2)}, u32[]{:S(2)}) collective-permute-start(bf16[4,4,8,4096]{3,2,1,0:T(8,128)(2,1)S(1)} %collective-permute-done.40), channel_id=1, source_target_pairs={{0,4},{1,5},{2,6},{3,7},{4,0},{5,1},{6,2},{7,3},{8,12},{9,13},{10,... | collective-permute-start | bytes 3145736 | tf_op jit(solution)/shard_map/gather_ff_in/ppermute | solution.py:35
  212.2 13.9 %collective-permute-start.56 = (bf16[4,4,32,1024]{3,2,1,0:T(8,128)(2,1)}, bf16[4,4,32,1024]{3,2,1,0:T(8,128)(2,1)S(1)}, u32[]{:S(2)}, u32[]{:S(2)}) collective-permute-start(bf16[4,4,32,1024]{3,2,1,0:T(8,128)(2,1)} %collective-permute-done.55), channel_id=1, source_target_pairs={{0,4},{1,5},{2,6},{3,7},{4,0},{5,1},{6,2},{7,3},{8,12},{9,13},{10,... | collective-permute-start | bytes 3145736 | tf_op jit(solution)/shard_map/gather_ff_out/ppermute | solution.py:35
  212.7 17.0 %collective-permute-start.58 = (bf16[2,4,32,1024]{3,2,1,0:T(8,128)(2,1)S(1)}, bf16[2,4,32,1024]{3,2,1,0:T(8,128)(2,1)S(1)}, u32[]{:S(2)}, u32[]{:S(2)}) collective-permute-start(bf16[2,4,32,1024]{3,2,1,0:T(8,128)(2,1)S(1)} %collective-permute-done.57), channel_id=1, source_target_pairs={{0,4},{1,5},{2,6},{3,7},{4,0},{5,1},{6,2},{7,3},{8,12},{9,13},{10,... | collective-permute-start | bytes 1572872 | tf_op jit(solution)/shard_map/gather_ff_out/ppermute | solution.py:35
  220.0 18.7 %collective-permute-start.60 = (bf16[2,4,32,1024]{3,2,1,0:T(8,128)(2,1)S(1)}, bf16[2,4,32,1024]{3,2,1,0:T(8,128)(2,1)S(1)}, u32[]{:S(2)}, u32[]{:S(2)}) collective-permute-start(bf16[2,4,32,1024]{3,2,1,0:T(8,128)(2,1)S(1)} %collective-permute-done.59), channel_id=1, source_target_pairs={{0,4},{1,5},{2,6},{3,7},{4,0},{5,1},{6,2},{7,3},{8,12},{9,13},{10,... | collective-permute-start | bytes 1572872 | tf_op jit(solution)/shard_map/gather_ff_out/ppermute | solution.py:35
  221.4 10.1 %collective-permute-start.45 = (bf16[2,4,8,4096]{3,2,1,0:T(8,128)(2,1)S(1)}, bf16[2,4,8,4096]{3,2,1,0:T(8,128)(2,1)S(1)}, u32[]{:S(2)}, u32[]{:S(2)}) collective-permute-start(bf16[2,4,8,4096]{3,2,1,0:T(8,128)(2,1)S(1)} %collective-permute-done.44), channel_id=1, source_target_pairs={{0,4},{1,5},{2,6},{3,7},{4,0},{5,1},{6,2},{7,3},{8,12},{9,13},{10,... | collective-permute-start | bytes 1572872 | tf_op jit(solution)/shard_map/gather_ff_in/ppermute | solution.py:35
  275.7 23.3 %collective-permute-start.63 = (bf16[256,256]{1,0:T(8,128)(2,1)S(1)}, bf16[256,256]{1,0:T(8,128)(2,1)}, u32[]{:S(2)}, u32[]{:S(2)}) collective-permute-start(bf16[256,256]{1,0:T(8,128)(2,1)S(1)} %bitcast.418), channel_id=1, source_target_pairs={{0,1},{1,2},{2,3},{3,0},{4,5},{5,6},{6,7},{7,4},{8,9},{9,10},{10,1... | collective-permute-start | bytes 393224 | tf_op jit(solution)/shard_map/attention_back/ppermute | solution.py:35
  275.8 23.2 %collective-permute-start.62 = (bf16[256,256]{1,0:T(8,128)(2,1)S(1)}, bf16[256,256]{1,0:T(8,128)(2,1)}, u32[]{:S(2)}, u32[]{:S(2)}) collective-permute-start(bf16[256,256]{1,0:T(8,128)(2,1)S(1)} %bitcast.419), channel_id=1, source_target_pairs={{0,2},{1,3},{2,0},{3,1},{4,6},{5,7},{6,4},{7,5},{8,10},{9,11},{10,... | collective-permute-start | bytes 393224 | tf_op jit(solution)/shard_map/attention_back/ppermute | solution.py:35
  277.6 21.4 %collective-permute-start.61 = (bf16[256,256]{1,0:T(8,128)(2,1)}, bf16[256,256]{1,0:T(8,128)(2,1)}, u32[]{:S(2)}, u32[]{:S(2)}) collective-permute-start(bf16[256,256]{1,0:T(8,128)(2,1)} %bitcast.387), channel_id=1, source_target_pairs={{0,3},{1,0},{2,1},{3,2},{4,7},{5,4},{6,5},{7,6},{8,11},{9,8},{10,9... | collective-permute-start | bytes 393224 | tf_op jit(solution)/shard_map/attention_back/ppermute | solution.py:35
  292.6 124.5 %collective-permute-start.87 = (bf16[4,4,4,8,4096]{4,3,2,0,1:T(8,128)(2,1)}, bf16[4,4,4,8,4096]{4,3,2,0,1:T(8,128)(2,1)}, u32[]{:S(2)}, u32[]{:S(2)}) collective-permute-start(bf16[4,4,4,8,4096]{4,3,2,0,1:T(8,128)(2,1)} %bitcast.383), channel_id=1, source_target_pairs={{0,4},{1,5},{2,6},{3,7},{4,0},{5,1},{6,2},{7,3},{8,12},{9,13},{10,... | collective-permute-start | bytes 12582920 | tf_op jit(solution)/shard_map/scatter_ff_in/ppermute | solution.py:35
  335.4 18.1 %collective-permute-start.66 = (bf16[256,1024]{1,0:T(8,128)(2,1)S(1)}, bf16[256,1024]{1,0:T(8,128)(2,1)S(1)}, u32[]{:S(2)}, u32[]{:S(2)}) collective-permute-start(bf16[256,1024]{1,0:T(8,128)(2,1)S(1)} %get-tuple-element.177), channel_id=1, source_target_pairs={{0,2},{1,3},{2,0},{3,1},{4,6},{5,7},{6,4},{7,5},{8,10},{9,11},{10,... | collective-permute-start | bytes 1572872 | tf_op jit(solution)/shard_map/input_grad/ppermute | solution.py:35
  339.2 11.6 %collective-permute-start.118 = (f32[12,1024]{1,0:T(8,128)S(1)}, f32[12,1024]{1,0:T(8,128)S(1)}, u32[]{:S(2)}, u32[]{:S(2)}) collective-permute-start(f32[12,1024]{1,0:T(8,128)S(1)} %add_add_fusion.3), channel_id=1, source_target_pairs={{0,3},{1,0},{2,1},{3,2},{4,7},{5,4},{6,5},{7,6},{8,11},{9,8},{10,9... | collective-permute-start | bytes 147464 | tf_op jit(solution)/shard_map/small_grads/ppermute | solution.py:35
  340.4 11.1 %collective-permute-start.117 = (f32[12,1024]{1,0:T(8,128)S(1)}, f32[12,1024]{1,0:T(8,128)S(1)}, u32[]{:S(2)}, u32[]{:S(2)}) collective-permute-start(f32[12,1024]{1,0:T(8,128)S(1)} %add_add_fusion.3), channel_id=1, source_target_pairs={{0,2},{1,3},{2,0},{3,1},{4,6},{5,7},{6,4},{7,5},{8,10},{9,11},{10,... | collective-permute-start | bytes 147464 | tf_op jit(solution)/shard_map/small_grads/ppermute | solution.py:35
  340.8 12.0 %collective-permute-start.116 = (f32[12,1024]{1,0:T(8,128)S(1)}, f32[12,1024]{1,0:T(8,128)S(1)}, u32[]{:S(2)}, u32[]{:S(2)}) collective-permute-start(f32[12,1024]{1,0:T(8,128)S(1)} %add_add_fusion.3), channel_id=1, source_target_pairs={{0,1},{1,2},{2,3},{3,0},{4,5},{5,6},{6,7},{7,4},{8,9},{9,10},{10,1... | collective-permute-start | bytes 147464 | tf_op jit(solution)/shard_map/small_grads/ppermute | solution.py:35
  350.8 13.8 %collective-permute-start.65 = (bf16[256,1024]{1,0:T(8,128)(2,1)S(1)}, bf16[256,1024]{1,0:T(8,128)(2,1)S(1)}, u32[]{:S(2)}, u32[]{:S(2)}) collective-permute-start(bf16[256,1024]{1,0:T(8,128)(2,1)S(1)} %get-tuple-element.178), channel_id=1, source_target_pairs={{0,3},{1,0},{2,1},{3,2},{4,7},{5,4},{6,5},{7,6},{8,11},{9,8},{10,9... | collective-permute-start | bytes 1572872 | tf_op jit(solution)/shard_map/input_grad/ppermute | solution.py:35
  351.5 13.8 %collective-permute-start.64 = (bf16[256,1024]{1,0:T(8,128)(2,1)S(1)}, bf16[256,1024]{1,0:T(8,128)(2,1)S(1)}, u32[]{:S(2)}, u32[]{:S(2)}) collective-permute-start(bf16[256,1024]{1,0:T(8,128)(2,1)S(1)} %get-tuple-element.176), channel_id=1, source_target_pairs={{0,1},{1,2},{2,3},{3,0},{4,5},{5,6},{6,7},{7,4},{8,9},{9,10},{10,1... | collective-permute-start | bytes 1572872 | tf_op jit(solution)/shard_map/input_grad/ppermute | solution.py:35
  352.8 13.9 %collective-permute-start.67 = (bf16[4,4,4,8,768]{4,3,2,1,0:T(8,128)(2,1)S(1)}, bf16[4,4,4,8,768]{4,3,2,1,0:T(8,128)(2,1)S(1)}, u32[]{:S(2)}, u32[]{:S(2)}) collective-permute-start(bf16[4,4,4,8,768]{4,3,2,1,0:T(8,128)(2,1)S(1)} %dynamic-slice_bitcast_fusion.1), channel_id=1, source_target_pairs={{0,4},{1,5},{2,6},{3,7},{4,0},{5,1},{6,2},{7,3},{8,12},{9,13},{10,... | collective-permute-start | bytes 2359304 | tf_op jit(solution)/shard_map/scatter_attn_in/ppermute | solution.py:35
  353.6 16.1 %collective-permute-start.77 = (bf16[4,4,4,8,1024]{4,3,0,1,2:T(8,128)(2,1)S(1)}, bf16[4,4,4,8,1024]{4,3,0,1,2:T(8,128)(2,1)S(1)}, u32[]{:S(2)}, u32[]{:S(2)}) collective-permute-start(bf16[4,4,4,8,1024]{4,3,0,1,2:T(8,128)(2,1)S(1)} %bitcast.411), channel_id=1, source_target_pairs={{0,4},{1,5},{2,6},{3,7},{4,0},{5,1},{6,2},{7,3},{8,12},{9,13},{10,... | collective-permute-start | bytes 3145736 | tf_op jit(solution)/shard_map/scatter_attn_out/ppermute | solution.py:35
  364.6 60.5 %collective-permute-start.98 = (bf16[4,4,4,32,1024]{4,3,2,1,0:T(8,128)(2,1)S(1)}, bf16[4,4,4,32,1024]{4,3,2,1,0:T(8,128)(2,1)}, u32[]{:S(2)}, u32[]{:S(2)}) collective-permute-start(bf16[4,4,4,32,1024]{4,3,2,1,0:T(8,128)(2,1)S(1)} %copy-done.9), channel_id=1, source_target_pairs={{0,4},{1,5},{2,6},{3,7},{4,0},{5,1},{6,2},{7,3},{8,12},{9,13},{10,... | collective-permute-start | bytes 12582920 | tf_op jit(solution)/shard_map/scatter_ff_out/ppermute | solution.py:35
  367.7 10.2 %collective-permute-start.69 = (bf16[4,4,8,768]{3,2,1,0:T(8,128)(2,1)S(1)}, bf16[4,4,8,768]{3,2,1,0:T(8,128)(2,1)S(1)}, u32[]{:S(2)}, u32[]{:S(2)}) collective-permute-start(bf16[4,4,8,768]{3,2,1,0:T(8,128)(2,1)S(1)} %get-tuple-element.193), channel_id=1, source_target_pairs={{0,24},{1,25},{2,26},{3,27},{4,28},{5,29},{6,30},{7,31},{8,0},{9,1... | collective-permute-start | bytes 589832 | tf_op jit(solution)/shard_map/scatter_attn_in/ppermute | solution.py:35
  392.3 10.5 %collective-permute-start.80 = (bf16[4,4,8,1024]{3,2,0,1:T(8,128)(2,1)S(1)}, bf16[4,4,8,1024]{3,2,0,1:T(8,128)(2,1)S(1)}, u32[]{:S(2)}, u32[]{:S(2)}) collective-permute-start(bf16[4,4,8,1024]{3,2,0,1:T(8,128)(2,1)S(1)} %get-tuple-element.189), channel_id=1, source_target_pairs={{0,2},{1,3},{2,0},{3,1},{4,6},{5,7},{6,4},{7,5},{8,10},{9,11},{10,... | collective-permute-start | bytes 786440 | tf_op jit(solution)/shard_map/scatter_attn_out/ppermute | solution.py:35
  394.7 10.8 %collective-permute-start.79 = (bf16[4,4,8,1024]{3,2,0,1:T(8,128)(2,1)S(1)}, bf16[4,4,8,1024]{3,2,0,1:T(8,128)(2,1)S(1)}, u32[]{:S(2)}, u32[]{:S(2)}) collective-permute-start(bf16[4,4,8,1024]{3,2,0,1:T(8,128)(2,1)S(1)} %get-tuple-element.190), channel_id=1, source_target_pairs={{0,3},{1,0},{2,1},{3,2},{4,7},{5,4},{6,5},{7,6},{8,11},{9,8},{10,9... | collective-permute-start | bytes 786440 | tf_op jit(solution)/shard_map/scatter_attn_out/ppermute | solution.py:35
  414.8 26.9 %collective-permute-start.86 = (bf16[8,1024]{1,0:T(8,128)(2,1)}, bf16[8,1024]{1,0:T(8,128)(2,1)}, u32[]{:S(2)}, u32[]{:S(2)}) collective-permute-start(bf16[8,1024]{1,0:T(8,128)(2,1)} %get-tuple-element.225), channel_id=1, source_target_pairs={{0,64},{1,65},{2,66},{3,67},{4,68},{5,69},{6,70},{7,71},{8,72},{9,... | collective-permute-start | bytes 49160 | tf_op jit(solution)/shard_map/scatter_attn_out/ppermute | solution.py:35
  421.9 13.1 %collective-permute-start.88 = (bf16[2,4,8,4096]{3,2,1,0:T(8,128)(2,1)}, bf16[2,4,8,4096]{3,2,1,0:T(8,128)(2,1)S(1)}, u32[]{:S(2)}, u32[]{:S(2)}) collective-permute-start(bf16[2,4,8,4096]{3,2,1,0:T(8,128)(2,1)} %get-tuple-element.170), channel_id=1, source_target_pairs={{0,8},{1,9},{2,10},{3,11},{4,12},{5,13},{6,14},{7,15},{8,16},{9,17... | collective-permute-start | bytes 1572872 | tf_op jit(solution)/shard_map/scatter_ff_in/ppermute | solution.py:35
  421.9 13.1 %collective-permute-start.90 = (bf16[2,4,8,4096]{3,2,1,0:T(8,128)(2,1)}, bf16[2,4,8,4096]{3,2,1,0:T(8,128)(2,1)}, u32[]{:S(2)}, u32[]{:S(2)}) collective-permute-start(bf16[2,4,8,4096]{3,2,1,0:T(8,128)(2,1)} %get-tuple-element.172), channel_id=1, source_target_pairs={{0,24},{1,25},{2,26},{3,27},{4,28},{5,29},{6,30},{7,31},{8,0},{9,1... | collective-permute-start | bytes 1572872 | tf_op jit(solution)/shard_map/scatter_ff_in/ppermute | solution.py:35
  431.4 20.5 %collective-permute-start.99 = (bf16[2,4,32,1024]{3,2,1,0:T(8,128)(2,1)}, bf16[2,4,32,1024]{3,2,1,0:T(8,128)(2,1)}, u32[]{:S(2)}, u32[]{:S(2)}) collective-permute-start(bf16[2,4,32,1024]{3,2,1,0:T(8,128)(2,1)} %get-tuple-element.164), channel_id=1, source_target_pairs={{0,32},{1,33},{2,34},{3,35},{4,36},{5,37},{6,38},{7,39},{8,40},{9,... | collective-permute-start | bytes 1572872 | tf_op jit(solution)/shard_map/scatter_ff_out/ppermute | solution.py:35
  433.3 18.7 %collective-permute-start.101 = (bf16[2,4,32,1024]{3,2,1,0:T(8,128)(2,1)}, bf16[2,4,32,1024]{3,2,1,0:T(8,128)(2,1)}, u32[]{:S(2)}, u32[]{:S(2)}) collective-permute-start(bf16[2,4,32,1024]{3,2,1,0:T(8,128)(2,1)} %get-tuple-element.166), channel_id=1, source_target_pairs={{0,96},{1,97},{2,98},{3,99},{4,100},{5,101},{6,102},{7,103},{8,104... | collective-permute-start | bytes 1572872 | tf_op jit(solution)/shard_map/scatter_ff_out/ppermute | solution.py:35
  437.5 22.6 %collective-permute-start.91 = (bf16[4,4,8,4096]{3,2,1,0:T(8,128)(2,1)}, bf16[4,4,8,4096]{3,2,1,0:T(8,128)(2,1)S(1)}, u32[]{:S(2)}, u32[]{:S(2)}) collective-permute-start(bf16[4,4,8,4096]{3,2,1,0:T(8,128)(2,1)} %pad_maximum_fusion.2), channel_id=1, source_target_pairs={{0,24},{1,25},{2,26},{3,27},{4,28},{5,29},{6,30},{7,31},{8,0},{9,1... | collective-permute-start | bytes 3145736 | tf_op jit(solution)/shard_map/scatter_ff_in/ppermute | solution.py:35
  441.7 22.9 %collective-permute-start.89 = (bf16[4,4,8,4096]{3,2,1,0:T(8,128)(2,1)}, bf16[4,4,8,4096]{3,2,1,0:T(8,128)(2,1)S(1)}, u32[]{:S(2)}, u32[]{:S(2)}) collective-permute-start(bf16[4,4,8,4096]{3,2,1,0:T(8,128)(2,1)} %pad_maximum_fusion.1), channel_id=1, source_target_pairs={{0,8},{1,9},{2,10},{3,11},{4,12},{5,13},{6,14},{7,15},{8,16},{9,17... | collective-permute-start | bytes 3145736 | tf_op jit(solution)/shard_map/scatter_ff_in/ppermute | solution.py:35
  454.0 25.9 %collective-permute-start.102 = (bf16[4,4,32,1024]{3,2,1,0:T(8,128)(2,1)S(1)}, bf16[4,4,32,1024]{3,2,1,0:T(8,128)(2,1)S(1)}, u32[]{:S(2)}, u32[]{:S(2)}) collective-permute-start(bf16[4,4,32,1024]{3,2,1,0:T(8,128)(2,1)S(1)} %pad_maximum_fusion.4), channel_id=1, source_target_pairs={{0,96},{1,97},{2,98},{3,99},{4,100},{5,101},{6,102},{7,103},{8,104... | collective-permute-start | bytes 3145736 | tf_op jit(solution)/shard_map/scatter_ff_out/ppermute | solution.py:35
  456.6 25.2 %collective-permute-start.100 = (bf16[4,4,32,1024]{3,2,1,0:T(8,128)(2,1)S(1)}, bf16[4,4,32,1024]{3,2,1,0:T(8,128)(2,1)S(1)}, u32[]{:S(2)}, u32[]{:S(2)}) collective-permute-start(bf16[4,4,32,1024]{3,2,1,0:T(8,128)(2,1)S(1)} %pad_maximum_fusion.3), channel_id=1, source_target_pairs={{0,32},{1,33},{2,34},{3,35},{4,36},{5,37},{6,38},{7,39},{8,40},{9,... | collective-permute-start | bytes 3145736 | tf_op jit(solution)/shard_map/scatter_ff_out/ppermute | solution.py:35
  466.3 20.4 %collective-permute-start.94 = (bf16[4,8,4096]{2,1,0:T(8,128)(2,1)S(1)}, bf16[4,8,4096]{2,1,0:T(8,128)(2,1)S(1)}, u32[]{:S(2)}, u32[]{:S(2)}) collective-permute-start(bf16[4,8,4096]{2,1,0:T(8,128)(2,1)S(1)} %get-tuple-element.186), channel_id=1, source_target_pairs={{0,64},{1,65},{2,66},{3,67},{4,68},{5,69},{6,70},{7,71},{8,72},{9,... | collective-permute-start | bytes 786440 | tf_op jit(solution)/shard_map/scatter_ff_in/ppermute | solution.py:35
  467.8 19.8 %collective-permute-start.93 = (bf16[4,8,4096]{2,1,0:T(8,128)(2,1)S(1)}, bf16[4,8,4096]{2,1,0:T(8,128)(2,1)S(1)}, u32[]{:S(2)}, u32[]{:S(2)}) collective-permute-start(bf16[4,8,4096]{2,1,0:T(8,128)(2,1)S(1)} %get-tuple-element.187), channel_id=1, source_target_pairs={{0,96},{1,97},{2,98},{3,99},{4,100},{5,101},{6,102},{7,103},{8,104... | collective-permute-start | bytes 786440 | tf_op jit(solution)/shard_map/scatter_ff_in/ppermute | solution.py:35
  470.2 17.4 %collective-permute-start.92 = (bf16[4,8,4096]{2,1,0:T(8,128)(2,1)S(1)}, bf16[4,8,4096]{2,1,0:T(8,128)(2,1)S(1)}, u32[]{:S(2)}, u32[]{:S(2)}) collective-permute-start(bf16[4,8,4096]{2,1,0:T(8,128)(2,1)S(1)} %get-tuple-element.185), channel_id=1, source_target_pairs={{0,32},{1,33},{2,34},{3,35},{4,36},{5,37},{6,38},{7,39},{8,40},{9,... | collective-permute-start | bytes 786440 | tf_op jit(solution)/shard_map/scatter_ff_in/ppermute | solution.py:35
  517.7 11.7 %collective-permute-start.123 = (f32[1,1]{1,0:T(1,128)}, f32[1,1]{1,0:T(1,128)}, u32[]{:S(2)}, u32[]{:S(2)}) collective-permute-start(f32[1,1]{1,0:T(1,128)} %add.1008), channel_id=1, source_target_pairs={{0,32},{1,33},{2,34},{3,35},{4,36},{5,37},{6,38},{7,39},{8,40},{9,... | collective-permute-start | bytes 20 | tf_op jit(solution)/shard_map/norm/ppermute | solution.py:35
  519.3 10.7 %collective-permute-start.124 = (f32[1,1]{1,0:T(1,128)}, f32[1,1]{1,0:T(1,128)}, u32[]{:S(2)}, u32[]{:S(2)}) collective-permute-start(f32[1,1]{1,0:T(1,128)} %add.1008), channel_id=1, source_target_pairs={{0,64},{1,65},{2,66},{3,67},{4,68},{5,69},{6,70},{7,71},{8,72},{9,... | collective-permute-start | bytes 20 | tf_op jit(solution)/shard_map/norm/ppermute | solution.py:35
  (141 other events, 2553.8 us)
